TPU v7x, 128 devices: a whole 4x4x4 slice. The times are simulated.
128 devices in a mesh: dp: 32 (over x, y, core), tensor: 4 (over z).
Axes of the slice: x: 4, y: 4, z: 4, core: 2. Of those that a mesh axis runs over, the one named last changes fastest.
Arguments:
- partial_grads: bfloat16 [32, 24, 1024, 1024], P('dp', 'tensor'), may hold values from -5 to 5
- owner_slots: int32 [24, 2], replicated, may hold values from 0 to 127, as said below
- statistics: float32 [32, 4, 1, 1024, 1024], P('dp', 'tensor'), may hold values from -6 to 6
- inv_roots: bfloat16 [32, 4, 1, 1024, 1024], P('dp', 'tensor'), may hold values from -0.1875 to 0.1875
Outputs:
- new_stats: float32 [32, 4, 1, 1024, 1024], P('dp', 'tensor')
- update: bfloat16 [24, 1024, 1024], P('tensor', 'dp')
Inputs may be any that keep to these rules, and one draw needn't show every extreme that they name: `owner_slots`: the 48 entries name distinct slots; some device has all 1 of its slots named.
All inputs are finite; a program needn't handle non-finite values.
Results may differ from a plain program's by a relative error of at most 0.024.
Values may be sent and summed in bfloat16 or wider, within the bound.
A program may use at most 128 MiB of HBM per device.

v0:
```python
import jax
import jax.numpy as jnp
from jax import lax
from jax.sharding import PartitionSpec as P

decay_rate = 0.9


def slot_matrix(owner_slots, column, slot_count):
    slot_ids = lax.broadcasted_iota(jnp.int32, (slot_count, owner_slots.shape[0]), 0)
    return (slot_ids == owner_slots[:, column][None, :]).astype(jnp.bfloat16)


def body(partial_grads, owner_slots, statistics, inv_roots):
    n_data = lax.axis_size("dp")
    n_tensor = lax.axis_size("tensor")
    data_index = lax.axis_index("dp")
    tensor_index = lax.axis_index("tensor")
    grad_parts = partial_grads[0]
    local_blocks = grad_parts.shape[0]
    block_width = grad_parts.shape[2]
    all_blocks = owner_slots.shape[0]
    capacity = statistics.shape[2]
    slot_count = n_data * n_tensor * capacity
    row_piece = block_width // n_data
    summed = lax.psum_scatter(
        grad_parts.astype(jnp.float32).astype(jnp.bfloat16), "dp", scatter_dimension=1, tiled=True
    )
    left_grid = slot_matrix(owner_slots, 0, slot_count).reshape(
        n_data, n_tensor, capacity, all_blocks
    )
    right_grid = slot_matrix(owner_slots, 1, slot_count).reshape(
        n_data, n_tensor, capacity, all_blocks
    )
    either_grid = left_grid + right_grid
    left_here = lax.dynamic_index_in_dim(left_grid, tensor_index, 1, False)
    right_here = lax.dynamic_index_in_dim(right_grid, tensor_index, 1, False)
    left_mine = lax.dynamic_index_in_dim(left_here, data_index, 0, False)
    right_mine = lax.dynamic_index_in_dim(right_here, data_index, 0, False)
    group_cols = lax.dynamic_slice_in_dim(either_grid, tensor_index * local_blocks, local_blocks, 3)
    outgoing = jnp.einsum(
        "dtci,iry->cdtry", group_cols, summed, preferred_element_type=jnp.float32
    ).astype(jnp.bfloat16)
    received = lax.all_to_all(
        lax.all_to_all(outgoing, "dp", split_axis=1, concat_axis=1, tiled=True),
        "tensor",
        split_axis=2,
        concat_axis=2,
        tiled=True,
    )
    owned_blocks = jnp.sum(received.astype(jnp.float32), axis=2).astype(jnp.bfloat16)
    owned_blocks = owned_blocks.reshape(capacity, block_width, block_width)
    is_left = jnp.sum(left_mine.astype(jnp.float32), axis=1)[:, None, None]
    is_right = jnp.sum(right_mine.astype(jnp.float32), axis=1)[:, None, None]
    turned = jnp.where(is_right > 0, jnp.swapaxes(owned_blocks, 1, 2), owned_blocks)
    gram_matrix = jnp.einsum(
        "cxk,cyk->cxy", turned, turned, preferred_element_type=jnp.float32
    ) * block_width ** (-0.5)
    old_stats = statistics[0, 0]
    blended = decay_rate * old_stats + (1 - decay_rate) * gram_matrix
    new_stats = jnp.where(is_left + is_right > 0, blended, old_stats)[None, None]
    slot_roots = inv_roots[0, 0]
    mixed = jnp.einsum(
        "cxk,cky->cxy", slot_roots, owned_blocks, preferred_element_type=jnp.float32
    ).astype(jnp.bfloat16)
    mixed_pieces = lax.all_to_all(
        mixed.reshape(capacity, n_data, row_piece, block_width),
        "dp",
        split_axis=1,
        concat_axis=1,
        tiled=True,
    )
    mixed_part = jnp.einsum(
        "scb,csry->bry", left_here, mixed_pieces, preferred_element_type=jnp.float32
    )
    mixed_all = lax.psum(mixed_part.astype(jnp.bfloat16), "tensor")
    outgoing_mixed = jnp.einsum(
        "dcb,bry->cdry", right_here, mixed_all, preferred_element_type=jnp.float32
    ).astype(jnp.bfloat16)
    mixed_full = lax.all_to_all(
        outgoing_mixed, "dp", split_axis=1, concat_axis=1, tiled=True
    ).reshape(capacity, block_width, block_width)
    precond = jnp.einsum(
        "cxk,cky->cxy", mixed_full, slot_roots, preferred_element_type=jnp.float32
    ).astype(jnp.bfloat16)
    precond_pieces = lax.all_to_all(
        precond.reshape(capacity, n_data, row_piece, block_width),
        "dp",
        split_axis=1,
        concat_axis=1,
        tiled=True,
    )
    precond_part = jnp.einsum(
        "scb,csry->bry", right_here, precond_pieces, preferred_element_type=jnp.float32
    )
    update = lax.psum_scatter(
        precond_part.astype(jnp.bfloat16), "tensor", scatter_dimension=0, tiled=True
    )
    return (new_stats, update)


def solution(mesh):
    return jax.shard_map(
        body,
        mesh=mesh,
        in_specs=(
            P("dp", "tensor", None, None),
            P(),
            P("dp", "tensor", None, None, None),
            P("dp", "tensor", None, None, None),
        ),
        out_specs=(P("dp", "tensor", None, None, None), P("tensor", "dp", None)),
        check_vma=False,
    )
```

profile of v0, /device:TPU:1, one launch (start us, length us, event | category | flops | bytes accessed | tf_op | source)
XLA Modules:
  0.0 544.8 jit_solution(4450054725336818723)
XLA Ops:
  8.1 110.1 %reduce-scatter.3.cloned.1.call-done = bf16[6,32,1024]{2,1,0:T(8,128)(2,1)} async-done(((bf16[6,1024,1024]{2,1,0:T(8,128)(2,1)}), bf16[6,32,1024]{2,1,0:T(8,128)(2,1)}) %reduce-scatter.3.cloned.1.call-update) | async-done | bytes 393232 | tf_op jit(solution)/shard_map/reduce_scatter | solution.py:26
  118.2 5.6 %convert_bitcast_fusion = bf16[1,32,4,32,1024]{4,1,3,2,0:T(8,128)(2,1)} fusion(bf16[6,32,1024]{2,1,0:T(8,128)(2,1)} %reduce-scatter.3.cloned.1.call-done, bf16[32,4,1,24]{0,3,1,2:T(8,128)(2,1)S(1)} %get-tuple-element.7, s32[]{:T(128)S(6)} %select_n.30, bf16[32,4,1,24]{0,3,1,2:T(8,128)(2,1)S(1)} %get-tuple-element.10), kind=kOutput, calls=%fused_computation.1 | convolution fusion | flops 54529024 | bytes 8798212 | tf_op jit(solution)/shard_map/dtci,iry->cdtry/dot_general | solution.py:41
  123.9 11.3 %copy.27 = bf16[1,32,4,32,1024]{4,3,2,0,1:T(8,128)(2,1)} copy(bf16[1,32,4,32,1024]{4,1,3,2,0:T(8,128)(2,1)} %convert_bitcast_fusion) | data formatting | bytes 16777216 | tf_op jit(solution)/shard_map/convert_element_type | solution.py:43
  135.2 102.4 %all_to_all.25 = bf16[1,32,4,32,1024]{4,3,2,0,1:T(8,128)(2,1)} all-to-all(bf16[1,32,4,32,1024]{4,3,2,0,1:T(8,128)(2,1)} %copy.27), channel_id=1, replica_groups=mesh['dp'=32,'tensor'=4] {'dp'}, dimensions={1} | all-to-all | bytes 16777216 | tf_op jit(solution)/shard_map/all_to_all | solution.py:45
  237.5 11.4 %copy.28 = bf16[1,32,4,32,1024]{4,1,3,0,2:T(8,128)(2,1)} copy(bf16[1,32,4,32,1024]{4,3,2,0,1:T(8,128)(2,1)} %all_to_all.25) | data formatting | bytes 16777216 | tf_op jit(solution)/shard_map/all_to_all | solution.py:45
  248.9 97.6 %all_to_all.26 = bf16[1,32,4,32,1024]{4,1,3,0,2:T(8,128)(2,1)S(1)} all-to-all(bf16[1,32,4,32,1024]{4,1,3,0,2:T(8,128)(2,1)} %copy.28), channel_id=1, replica_groups=mesh['dp'=32,'tensor'=4] {'tensor'}, dimensions={2} | all-to-all | bytes 16777216 | tf_op jit(solution)/shard_map/all_to_all | solution.py:44
  346.5 2.1 bitcast_reduce_fusion
  348.6 1.2 copy.30
  349.8 3.7 fusion.14
  353.5 5.6 %all-to-all-start.2 = ((bf16[1,32,32,1024]{3,2,0,1:T(8,128)(2,1)}), bf16[1,32,32,1024]{3,2,0,1:T(8,128)(2,1)}, u32[]{:S(2)}, u32[]{:S(2)}) async-start(bf16[1,32,32,1024]{3,2,0,1:T(8,128)(2,1)} %bitcast.94), calls=%async_computation.3 | async-start | bytes 4194304 | tf_op jit(solution)/shard_map/all_to_all | solution.py:66
  359.4 28.2 %all-to-all-done.2 = bf16[1,32,32,1024]{3,2,0,1:T(8,128)(2,1)} async-done(((bf16[1,32,32,1024]{3,2,0,1:T(8,128)(2,1)}), bf16[1,32,32,1024]{3,2,0,1:T(8,128)(2,1)}, u32[]{:S(2)}, u32[]{:S(2)}) %all-to-all-start.2) | async-done | bytes 2097184 | tf_op jit(solution)/shard_map/all_to_all | solution.py:66
  387.6 5.1 fusion.20
  392.7 46.2 %all-reduce.2.cloned.1.call-done = bf16[24,32,1024]{2,0,1:T(8,128)(2,1)} async-done(((bf16[24,32,1024]{2,0,1:T(8,128)(2,1)}), bf16[24,32,1024]{2,0,1:T(8,128)(2,1)}) %all-reduce.2.cloned.1.call-update) | async-done | bytes 1572880 | tf_op jit(solution)/shard_map/psum | solution.py:76
  439.0 2.2 convert_bitcast_fusion.1
  441.2 1.2 copy.35
  442.3 35.6 %all_to_all.27 = bf16[1,32,32,1024]{3,2,0,1:T(8,128)(2,1)S(1)} all-to-all(bf16[1,32,32,1024]{3,2,0,1:T(8,128)(2,1)S(1)} %copy.35), channel_id=1, replica_groups=mesh['dp'=32,'tensor'=4] {'dp'}, dimensions={1} | all-to-all | bytes 4194304 | tf_op jit(solution)/shard_map/all_to_all | solution.py:80
  478.0 2.3 fusion.17
  480.3 31.9 %all_to_all.28 = bf16[1,32,32,1024]{3,2,0,1:T(8,128)(2,1)S(1)} all-to-all(bf16[1,32,32,1024]{3,2,0,1:T(8,128)(2,1)S(1)} %bitcast.96), channel_id=1, replica_groups=mesh['dp'=32,'tensor'=4] {'dp'}, dimensions={1} | all-to-all | bytes 4194304 | tf_op jit(solution)/shard_map/all_to_all | solution.py:86
  512.2 2.4 fusion.23
  514.6 2.0 copy.38
  518.0 0.7 convert_reduce_fusion.1
  520.0 4.0 copy.31
  524.0 8.1 %fusion.1 = f32[1,1,1,1024,1024]{4,3,2,1,0:T(8,128)} fusion(f32[1,1,1,1024,1024]{4,3,2,1,0:T(8,128)} %param.6, bf16[1,1024,1024]{2,1,0:T(8,128)(2,1)} %bitcast.93, bf16[1,1024,1024]{1,2,0:T(8,128)(2,1)} %copy.31, pred[]{:T(512)S(6)} %gt.9, pred[]{:T(512)S(6)} %gt.8), kind=kOutput, calls=%fused_computation.5 | convolution fusion | flops 2152726528 | bytes 12582914 | tf_op jit(solution)/shard_map/cxk,cyk->cxy/dot_general | solution.py:56
  532.0 6.3 %reduce-scatter.5.cloned.1.call-done = bf16[6,32,1024]{2,1,0:T(8,128)(2,1)} async-done(((bf16[24,32,1024]{2,1,0:T(8,128)(2,1)}), bf16[6,32,1024]{2,1,0:T(8,128)(2,1)}) %reduce-scatter.5.cloned.1.call-update) | async-done | bytes 393232 | tf_op jit(solution)/shard_map/reduce_scatter | solution.py:96
  (16 shorter events, 2.0 us)
Async XLA Ops:
  7.2 342.7 %copy-start = (bf16[1,1,1,1024,1024]{4,3,2,1,0:T(8,128)(2,1)S(1)}, bf16[1,1,1,1024,1024]{4,3,2,1,0:T(8,128)(2,1)}, u32[]{:S(2)}) copy-start(bf16[1,1,1,1024,1024]{4,3,2,1,0:T(8,128)(2,1)} %param.7) | copy-start | bytes 6291460
  7.2 111.1 %reduce-scatter.3.cloned.1.call-start = ((), (), s32[]{:S(2)}) async-start(), calls=%async_computation.7 | async-start | bytes 12976128 | tf_op jit(solution)/shard_map/reduce_scatter | solution.py:26
  7.2 0.8 copy-start.2
  349.8 3.7 copy-start.1
  353.5 34.1 %all-to-all-start.2 = ((bf16[1,32,32,1024]{3,2,0,1:T(8,128)(2,1)}), bf16[1,32,32,1024]{3,2,0,1:T(8,128)(2,1)}, u32[]{:S(2)}, u32[]{:S(2)}) async-start(bf16[1,32,32,1024]{3,2,0,1:T(8,128)(2,1)} %bitcast.94), calls=%async_computation.3 | async-start | bytes 4194304 | tf_op jit(solution)/shard_map/all_to_all | solution.py:66
  359.1 79.8 %all-reduce.2.cloned.1.call-start = ((), (), s32[]{:S(2)}) async-start(), calls=%async_computation.8 | async-start | bytes 3145728 | tf_op jit(solution)/shard_map/psum | solution.py:76
  392.7 145.6 %reduce-scatter.5.cloned.1.call-start = ((), (), s32[]{:S(2)}) async-start(), calls=%async_computation.9 | async-start | bytes 1966080 | tf_op jit(solution)/shard_map/reduce_scatter | solution.py:96
Sparse Core Ops, SparseCore 0:
  11.8 106.3 reduce-scatter.2
  392.8 46.1 all-reduce.1
  516.8 21.4 reduce-scatter.4
where the time goes:
time: 546 us; the launch traced here: 545 us
  blocking collectives  267 us (49%)
  waiting for transfers between devices  191 us (35%)
  local copies, waits for them, and re-layouts  31.2 us (6%)
  matrix products  29.4 us (5%)
  between operations  15.8 us (3%)
  starting transfers between devices  5.96 us (1%)
    reduce_scatter x1, waiting for transfers between devices, body(): lax.psum_scatter(grad_parts.astype(jnp.float32).astype(jnp.bfloat16), 'dp...  110 us
    all_to_all x1, blocking collectives, body(): lax.all_to_all(outgoing, 'dp', split_axis=1, concat_axis=1, tiled=True)  102 us
    all_to_all x1, blocking collectives, body(): lax.all_to_all(lax.all_to_all(outgoing, 'dp', split_axis=1, concat_axis=1...  97.6 us
    psum x1, waiting for transfers between devices, body(): mixed_all = lax.psum(mixed_part.astype(jnp.bfloat16), 'tensor')  46.2 us
    all_to_all x1, blocking collectives, body(): lax.all_to_all(outgoing_mixed, 'dp', split_axis=1, concat_axis=1, tiled=T...  35.6 us
    all_to_all x1, blocking collectives, body(): lax.all_to_all(precond.reshape(capacity, n_data, row_piece, block_width),...  31.9 us
    all_to_all x1, waiting for transfers between devices, body(): lax.all_to_all(mixed.reshape(capacity, n_data, row_piece, block_width), '...  28.2 us
    all_to_all x1, local copies, waits for them, and re-layouts, body(): lax.all_to_all(outgoing, 'dp', split_axis=1, concat_axis=1, tiled=True)  11.4 us
  transfers between devices with their start and end apart: 4, of which 4 were waited for; matrix products, arithmetic and copies ran while one was open for 2% of the time, Pallas kernels for 0%

commit v1 on v0

v1 whole, which is shorter than its diff:
```python
import functools

import jax
import jax.numpy as jnp
from jax import lax
from jax.experimental import pallas as pl
from jax.experimental.pallas import tpu as pltpu
from jax.sharding import PartitionSpec as P

decay_rate = 0.9
MESH = pl.DeviceIdType.MESH
f32 = jnp.float32
bf16 = jnp.bfloat16
lo, hi = pl.ds(0, 3), pl.ds(3, 3)


def place():
    d = lax.axis_index("dp")
    return lax.div(d, 8), lax.rem(lax.div(d, 2), 4), lax.rem(d, 2), lax.axis_index("tensor")


def wrap(v):
    return lax.rem(v + 8, 4)


def remote(src, dst, send, recv, device):
    return pltpu.make_async_remote_copy(
        src_ref=src, dst_ref=dst, send_sem=send, recv_sem=recv, device_id=device, device_id_type=MESH
    )


class Net:
    def __init__(self, send, recv):
        self.x, self.y, self.c, self.t = place()
        self.send, self.recv, self.count, self.open = send, recv, 0, []
        self.at = {"x": self.x, "y": self.y, "z": self.t}
        self.pair = ((self.x * 4 + self.y) * 2 + 1 - self.c, self.t)

    def near(self, axis, step, swap=0):
        x, y, t = [wrap(self.at[a] + step) if a == axis else self.at[a] for a in "xyz"]
        return ((x * 4 + y) * 2 + (1 - self.c if swap else self.c), t)

    def greet(self):
        barrier = pltpu.get_barrier_semaphore()
        peers = [self.pair] + [self.near(axis, step) for axis in "xyz" for step in (1, -1)]
        peers += [self.near(axis, step, 1) for axis in "xy" for step in (1, -1)]
        for peer in peers:
            pl.semaphore_signal(barrier, inc=1, device_id=peer, device_id_type=MESH)
        pl.semaphore_wait(barrier, len(peers))

    def make(self, src, dst, device):
        copy = remote(src, dst, self.send.at[self.count], self.recv.at[self.count], device)
        self.count += 1
        return copy

    def start(self, src, dst, device, when=None):
        copy = self.make(src, dst, device)
        if when is None:
            copy.start()
        else:
            pl.when(when)(copy.start)
        self.open.append((copy, when))
        return copy

    def local(self, src, dst):
        copy = pltpu.make_async_copy(src, dst, self.send.at[self.count])
        self.count += 1
        copy.start()
        return copy

    def close(self):
        for copy, when in self.open:
            if when is None:
                copy.wait_send()
            else:
                pl.when(when)(copy.wait_send)


class Exchange:
    def __init__(self, net, axis, src, dst, relay):
        self.net, self.axis, self.dst, self.relay = net, axis, dst, relay
        here = net.at[axis]
        self.i = [wrap(here + o) for o in range(4)]
        right, left = net.near(axis, 1), net.near(axis, -1)
        self.far = [
            net.start(src(self.i[2], 0), relay.at[0], right),
            net.start(src(self.i[2], 1), relay.at[1], left),
        ]
        self.own = net.local(src(self.i[0], None), dst(self.i[0], None))
        self.direct = [
            net.start(src(self.i[1], None), dst(self.i[0], None), right),
            net.start(src(self.i[3], None), dst(self.i[0], None), left),
        ]

        self.passed = []

    def forward(self, way):
        self.far[way].wait_recv()
        source = self.i[3 if way == 0 else 1]
        self.passed.append(
            self.net.start(self.relay.at[way], self.dst(source, way), self.net.near(self.axis, 1 - 2 * way))
        )

    def finish(self):
        self.own.wait()
        for copy in self.direct + self.passed:
            copy.wait_recv()


def half(h):
    return slice(None) if h is None else pl.ds(2 * h, 2)


class LastLeg:
    def __init__(self, net, axis, src, dst, relay):
        self.net, self.axis, self.dst, self.relay = net, axis, dst, relay
        here = net.at[axis]
        self.i = [wrap(here + o) for o in range(4)]
        self.cores = [net.c, 1 - net.c]
        every = slice(None)
        self.far = [
            net.start(src(self.i[2], way, every), relay.at[way], net.near(axis, 1 - 2 * way)) for way in range(2)
        ]
        self.arrive = [
            net.start(src(self.i[o], None, self.cores[k]), dst(self.i[0], None), net.near(axis, step, k))
            for o, step in ((1, 1), (3, -1))
            for k in range(2)
        ]
        self.own = net.local(src(self.i[0], None, self.cores[0]), dst(self.i[0], None))
        self.arrive.append(net.start(src(self.i[0], None, self.cores[1]), dst(self.i[0], None), net.pair))

    def forward(self, way):
        net = self.net
        source = self.i[3 if way == 0 else 1]
        self.far[way].wait_recv()
        self.arrive += [
            net.start(
                self.relay.at[way, :, self.cores[k]], self.dst(source, way), net.near(self.axis, 1 - 2 * way, k)
            )
            for k in range(2)
        ]

    def finish(self):
        self.own.wait()
        for copy in self.arrive:
            copy.wait_recv()


class PlaneExchange:
    def __init__(self, net, parcels, middle, landing, relay):
        self.net, self.parcels, self.middle, self.landing, self.relay = net, parcels, middle, landing, relay
        self.legs = {}

    def first(self, s):
        a, d = self.parcels, self.middle

        def parcels(i, h):
            return a(0, i, half(h)) if s == 0 else a(1, half(h), i)

        self.legs[0, s] = Exchange(
            self.net, "xy"[s], parcels, lambda i, h: d.at[s, i, half(h)], self.relay.at[0, s]
        )

    def second(self, s):
        d, z, c = self.middle, self.landing, self.net.c
        self.legs[0, s].finish()

        def land(j, h):
            return z.at[half(h), j, c, 0] if s == 0 else z.at[j, half(h), c, 1]

        self.legs[1, s] = LastLeg(
            self.net, "yx"[s], lambda j, h, k: d.at[s, half(h), j, k], land, self.relay.at[1, s]
        )

    def finish(self):
        for s in range(2):
            self.legs[1, s].finish()


class WorkerLeg:
    def __init__(self, net, s, source, target, relay):
        self.net, self.s, self.axis = net, s, "xy"[s]
        here = net.at[self.axis]
        self.target, self.relay = target, relay
        self.i = i = [wrap(here + o) for o in range(4)]
        self.two = [v < 2 if s == 0 else v >= 2 for v in i]
        wide = relay.shape[-1]
        self.cols = [pl.ds(0, wide), pl.ds(wide, wide)]

        def when(o, rank):
            return self.two[o] if rank else None

        self.when = when
        self.far = [
            [
                net.start(
                    source.at[i[2], :, rank, :, self.cols[way]],
                    relay.at[way, :, rank],
                    net.near(self.axis, 1 - 2 * way),
                    when(2, rank),
                )
                for way in range(2)
            ]
            for rank in range(2)
        ]
        self.direct = [
            [
                net.start(
                    source.at[i[o], :, rank], target.at[:, i[0], rank], net.near(self.axis, step), when(o, rank)
                )
                for o, step in ((1, 1), (3, -1))
            ]
            for rank in range(2)
        ]
        self.own = net.local(source.at[i[0]], target.at[:, i[0]])
        self.passed = [[], []]

    def forward(self, way):
        o, goal = ((3, 1), (1, 3))[way]
        for rank in range(2):
            arrived = self.far[rank][way]
            when = self.when(goal, rank)
            if when is None:
                arrived.wait_recv()
            else:
                pl.when(when)(arrived.wait_recv)
            self.passed[rank].append(
                self.net.start(
                    self.relay.at[way, :, rank],
                    self.target.at[:, self.i[o], rank, :, self.cols[way]],
                    self.net.near(self.axis, 1 - 2 * way),
                    when,
                )
            )

    def finish(self):
        self.own.wait()
        for copy in self.direct[0] + self.passed[0]:
            copy.wait_recv()

        @pl.when(self.two[0])
        def _():
            for copy in self.direct[1] + self.passed[1]:
                copy.wait_recv()


class HomeLeg:
    def __init__(self, net, s, back, home, relay):
        self.net, self.axis, self.home, self.relay = net, "xy"[s], home, relay
        here = net.at[self.axis]
        self.i = i = [wrap(here + o) for o in range(4)]
        self.two = [v < 2 if s == 0 else v >= 2 for v in i]
        wide = relay.shape[-1]
        self.cols = [pl.ds(0, wide), pl.ds(wide, wide)]
        self.far = [
            [
                net.start(
                    back.at[rank, i[2], :, self.cols[way]],
                    relay.at[way, rank],
                    net.near(self.axis, 1 - 2 * way),
                    self.when(0, rank),
                )
                for way in range(2)
            ]
            for rank in range(2)
        ]
        self.direct = [
            [
                net.start(back.at[rank, i[o]], home.at[i[0], rank], net.near(self.axis, step), self.when(0, rank))
                for o, step in ((1, 1), (3, -1))
            ]
            for rank in range(2)
        ]
        self.own = net.local(back.at[:, i[0]], home.at[i[0]])
        self.passed = [[], []]

    def when(self, o, rank):
        return self.two[o] if rank else None

    def arrived(self, copy, o, rank):
        if rank:
            pl.when(self.two[o])(copy.wait_recv)
        else:
            copy.wait_recv()

    def forward(self, way):
        o = (3, 1)[way]
        for rank in range(2):
            self.arrived(self.far[rank][way], o, rank)
            self.passed[rank].append(
                self.net.start(
                    self.relay.at[way, rank],
                    self.home.at[self.i[o], rank, :, self.cols[way]],
                    self.net.near(self.axis, 1 - 2 * way),
                    self.when(o, rank),
                )
            )

    def finish(self):
        self.own.wait()
        for rank in range(2):
            for copy, o in zip(self.direct[rank] + self.passed[rank], (3, 1, 2, 2)):
                self.arrived(copy, o, rank)


def spot(s, block):
    if block < 4:
        return block, 0
    return (block - 4, 1) if s == 0 else (block - 2, 1)


class Workers:
    def __init__(self, net):
        self.net = net
        self.is_worker = lax.rem(net.x - net.y + 4, 2) == 0
        self.is_other = lax.rem(net.x - net.y + 4, 2) == 1
        self.ij = [(net.x, net.y), (net.y, net.x)]
        self.axes = ["y", "x"]

    def rank(self, s, step):
        i, j = self.ij[s]
        return lax.div(wrap(j + step - i), 2)

    def beside(self, s):
        return self.net.near(self.axes[s], 1), self.net.near(self.axes[s], -1)


class Gather:
    def __init__(self, w, s, unit, land, relay):
        self.w, net = w, w.net
        right, left = w.beside(s)
        j = [wrap(w.ij[s][1] + o) for o in range(4)]
        self.far = [
            net.make(unit(w.rank(s, 2), 0), relay.at[0], right),
            net.make(unit(w.rank(s, 2), 1), relay.at[1], left),
        ]
        self.direct = [
            net.make(unit(w.rank(s, 1), None), land(j[0], None), right),
            net.make(unit(w.rank(s, 3), None), land(j[0], None), left),
        ]
        self.passed = [
            net.make(relay.at[0], land(j[3], 0), right),
            net.make(relay.at[1], land(j[1], 1), left),
        ]
        self.own = pltpu.make_async_copy(unit(w.rank(s, 0), None), land(j[0], None), net.send.at[net.count])
        net.count += 1

        @pl.when(w.is_worker)
        def _():
            for copy in self.far + [self.own]:
                copy.start()

        @pl.when(w.is_other)
        def _():
            for copy in self.direct:
                copy.start()

        net.open += [(copy, w.is_worker) for copy in self.far]
        net.open += [(copy, w.is_other) for copy in self.direct + self.passed]

    def forward(self):
        @pl.when(self.w.is_other)
        def _():
            for arrived, onward in zip(self.far, self.passed):
                arrived.wait_recv()
                onward.start()

    def wait_here(self):
        self.own.wait()
        for copy in self.direct + self.passed:
            copy.wait_recv()


class Spread:
    def __init__(self, w, s, unit, land, relay):
        self.w, net = w, w.net
        right, left = w.beside(s)
        j = [wrap(w.ij[s][1] + o) for o in range(4)]
        mine = w.rank(s, 0)
        self.far = [net.make(unit(j[2], 0), relay.at[0], right), net.make(unit(j[2], 1), relay.at[1], left)]
        self.direct = [
            net.make(unit(j[1], None), land(mine, None), right),
            net.make(unit(j[3], None), land(mine, None), left),
        ]
        self.passed = [
            net.make(relay.at[0], land(w.rank(s, 3), 0), right),
            net.make(relay.at[1], land(w.rank(s, 1), 1), left),
        ]
        self.own = pltpu.make_async_copy(unit(j[0], None), land(mine, None), net.send.at[net.count])
        net.count += 1

        @pl.when(w.is_worker)
        def _():
            for copy in self.far + self.direct + [self.own]:
                copy.start()

        net.open += [(copy, w.is_worker) for copy in self.far + self.direct]
        net.open += [(copy, w.is_other) for copy in self.passed]

    def forward(self):
        @pl.when(self.w.is_other)
        def _():
            for arrived, onward in zip(self.far, self.passed):
                arrived.wait_recv()
                onward.start()

    def finish(self):
        @pl.when(self.w.is_other)
        def _():
            for copy in self.direct:
                copy.wait_recv()

        @pl.when(self.w.is_worker)
        def _():
            self.own.wait()
            for copy in self.passed:
                copy.wait_recv()


class ReduceScatter:
    def __init__(self, net, parts, v):
        self.net, self.parts, self.v = net, parts, v
        at = [(net.x, net.y), (net.y, net.x)]
        self.i = [[wrap(at[s][0] + o) for o in range(4)] for s in range(2)]
        self.j = [[wrap(at[s][1] + o) for o in range(4)] for s in range(2)]
        self.loads, self.swaps, self.copies = {}, {}, {}

    def fetch(self, order):
        net, own, cin = self.net, self.v["own"], self.v["cin"]

        def view(s, i, core):
            return self.parts.at[:, i, :, core, 0] if s == 0 else self.parts.at[:, :, i, core, 1]

        for o in order:
            for s in range(2):
                i = self.i[s][o]
                self.swaps[s, o] = net.start(view(s, i, 1 - net.c), cin.at[s, i], net.pair)
                self.loads[s, o] = net.local(view(s, i, net.c), own.at[s, i])

    def ship(self, stage, s, way, src, dst):
        axis = "xy"[s] if stage < 3 else "yx"[s]
        self.copies[stage, s, way] = self.net.start(src, dst, self.net.near(axis, 1 - 2 * way))

    def ready(self, s, o):
        self.loads[s, o].wait()
        self.swaps[s, o].wait_recv()

    def add(self, out, terms, blocks):
        @pl.loop(0, blocks)
        def _(b):
            for j in range(4):
                total = terms[0][b, j].astype(f32)
                for term in terms[1:]:
                    total = total + term[b, j].astype(f32)
                out[b, j] = total.astype(bf16)

    def far(self, s):
        own, cin, first_in = self.v["own"], self.v["cin"], self.v["first_in"]
        i = self.i[s][2]
        self.ready(s, 2)
        self.add(own.at[s, i], [own.at[s, i], cin.at[s, i]], 6)
        self.ship(0, s, 0, own.at[s, i, lo], first_in.at[0, s, 0])
        self.ship(0, s, 1, own.at[s, i, hi], first_in.at[0, s, 1])

    def plain(self, way, s):
        own, cin, first_in = self.v["own"], self.v["cin"], self.v["first_in"]
        o, part = ((1, hi), (3, lo))[way]
        i = self.i[s][o]
        self.ready(s, o)
        self.add(own.at[s, i, part], [own.at[s, i, part], cin.at[s, i, part]], 3)
        self.ship(1, s, way, own.at[s, i, part], first_in.at[1, s, way])

    def merged(self, way, s):
        own, cin, first_in = self.v["own"], self.v["cin"], self.v["first_in"]
        o, part = ((1, lo), (3, hi))[way]
        i = self.i[s][o]
        self.copies[0, s, way].wait_recv()
        terms = [own.at[s, i, part], cin.at[s, i, part], first_in.at[0, s, way]]
        self.add(own.at[s, i, part], terms, 3)
        self.ship(2, s, way, own.at[s, i, part], first_in.at[2, s, way])

    def first_sum(self, s, j, b):
        own, cin, first_in = self.v["own"], self.v["cin"], self.v["first_in"]
        i = self.i[s][0]
        total = own[s, i, b, j].astype(f32) + cin[s, i, b, j].astype(f32)
        k, low = (b, 0) if b < 3 else (b - 3, 1)
        for stage, way in ((2, low), (1, 1 - low)):
            total = total + first_in[stage, s, way, k, j].astype(f32)
        return total

    def second(self, s):
        f, second_in = self.v["f"], self.v["second_in"]
        self.ready(s, 0)
        for stage in (1, 2):
            for way in range(2):
                self.copies[stage, s, way].wait_recv()
        j = self.j[s][2]
        for b in range(6):
            f[s, j, b] = self.first_sum(s, j, b).astype(bf16)
        self.ship(3, s, 0, f.at[s, j, lo], second_in.at[0, s, 0])
        self.ship(3, s, 1, f.at[s, j, hi], second_in.at[0, s, 1])

    def second_plain(self, way, s):
        f, second_in = self.v["f"], self.v["second_in"]
        o, part = ((1, hi), (3, lo))[way]
        j = self.j[s][o]
        for b in range(6):
            f[s, j, b] = self.first_sum(s, j, b).astype(bf16)
        self.ship(4, s, way, f.at[s, j, part], second_in.at[1, s, way])

    def second_merged(self, way, s):
        f, second_in = self.v["f"], self.v["second_in"]
        o, part, start = ((1, lo, 0), (3, hi, 3))[way]
        j = self.j[s][o]
        self.copies[3, s, way].wait_recv()
        for k in range(3):
            total = f[s, j, start + k].astype(f32) + second_in[0, s, way, k].astype(f32)
            f[s, j, start + k] = total.astype(bf16)
        self.ship(5, s, way, f.at[s, j, part], second_in.at[2, s, way])

    def finish(self, s, out):
        second_in = self.v["second_in"]
        for stage in (4, 5):
            for way in range(2):
                self.copies[stage, s, way].wait_recv()
        j = self.j[s][0]
        for b in range(6):
            total = self.first_sum(s, j, b)
            k, low = (b, 0) if b < 3 else (b - 3, 1)
            total = total + second_in[2, s, low, k].astype(f32)
            total = total + second_in[1, s, 1 - low, k].astype(f32)
            out[b, s] = total.astype(bf16)


(
    BLK, FAR, FETCH, G, GG, GGF, GL, GLF, MERGED, MMA, MMB, OW1, OW1F, OW2, OW2F, OWE, PLAIN, RG, RGF, RL, RLF,
    RO1, RO1F, RO2, RO2F, SEC, SECM, SECP, SH0, SH1, SP, SPF, UL, ULE, ULF, ZAF, ZF, ZM, ZP, ZSEL,
) = range(40)
ORDER = (
    (RO1, 1), (RO1, 0), (BLK,), (RO1F, 1, 1), (RO1F, 0, 1), (RO1F, 1, 0), (RO1F, 0, 0), (FETCH,), (RO2, 1),
    (RO2, 0), (RO2F, 0, 0), (RO2F, 1, 1), (RO2F, 1, 0), (FAR, 0), (PLAIN, 0, 0), (RO2F, 0, 1), (FAR, 1), (ZF,),
    (PLAIN, 1, 0), (PLAIN, 0, 1), (PLAIN, 1, 1), (ZP,), (ZM, 1), (MERGED, 0, 1), (MERGED, 1, 0),
    (MERGED, 0, 0), (MERGED, 1, 1), (ZM, 0), (SEC, 0), (SEC, 1), (SECP, 1, 1), (SECP, 0, 0), (SECP, 1, 0),
    (SECP, 0, 1), (ZSEL,), (SECM, 0, 0), (SECM, 1, 0), (SECM, 1, 1), (SECM, 0, 1), (RL, 1), (RL, 0), (G, 0),
    (G, 1), (GL, 0), (RLF, 1, 1), (GL, 1), (RLF, 1, 0), (GLF, 1, 0), (GLF, 0, 0), (RLF, 0, 0), (GLF, 0, 1),
    (GLF, 1, 1), (RLF, 0, 1), (RG, 1), (GG, 0), (GGF, 0), (ZAF, 0, 0), (ZAF, 0, 1), (ZAF, 1, 1), (RG, 0),
    (GG, 1), (GGF, 1), (ZAF, 1, 0), (RGF, 1), (OW1, 0), (RGF, 0), (OW1, 1), (SH0,), (SH1,), (MMA,),
    (OW1F, 0, 0), (OW1F, 0, 1), (OW1F, 1, 0), (OW1F, 1, 1), (MMB,), (SP,), (SPF, 0), (SPF, 1), (OW2, 1),
    (OW2, 0), (UL, 0), (OW2F, 1, 0), (UL, 1), (ULF, 0, 1), (ULF, 1, 0), (ULF, 0, 0), (OW2F, 0, 0), (ULF, 1, 1),
    (OW2F, 1, 1), (OW2F, 0, 1), (ULE,), (OWE,),
)


def step_kernel(names, *refs):
    v = dict(zip(names, refs))
    net = Net(v["send"], v["recv"])
    t, c = net.t, net.c
    owners, g, root, blocks = v["owners"], v["g"], v["root"], v["blocks"]
    every = [v["every_0"], v["every_1"]]
    net.greet()
    right, left = net.near("z", 1), net.near("z", -1)
    plane = [wrap(t + o) for o in range(4)]
    sums = ReduceScatter(net, v["parts"], v)
    workers = Workers(net)
    steps, kept = {}, {}

    def step(name):
        def keep(function):
            steps[name] = function

        return keep

    @step((FETCH,))
    def _():
        sums.fetch((2, 1, 3, 0))

    @step((BLK,))
    def _():
        @pl.loop(0, 32)
        def _(d):
            slot, block = d * 4 + t, jnp.int32(0)
            for b in range(24):
                hit = jnp.logical_or(owners[0, b] == slot, owners[1, b] == slot)
                block = jnp.where(hit, b, block)
            blocks[d] = block

    roots = PlaneExchange(
        net, lambda s, x, y: root.at[x, y, :, s], v["root_middle"], v["roots"], v["root_relay"]
    )
    parcels = v["owned_parcels"]
    owned = PlaneExchange(
        net, lambda s, x, y: parcels.at[s, x, y], v["owned_middle"], v["owned"], v["owned_relay"]
    )

    def pack_owned(s):
        kept["g_own", s].wait()
        for way in range(2):
            kept["g_pass", s, way].wait_recv()

        @pl.loop(0, 16)
        def _(chip):
            x, y = lax.div(chip, 4), lax.rem(chip, 4)
            for core in range(2):
                block = blocks[2 * chip + core]
                parcels[s, x, y, core] = every[s][lax.div(block, 6), lax.rem(block, 6)]

        owned.first(s)

    pieces, hold = v["roots"], v["hold"]
    far_in, plain_in, merged_in = v["z_far"], v["z_plain"], v["z_merged"]
    first_k, last_k = pl.ds(0, 6), pl.ds(6, 6)

    def wanted(target, k):
        slot = owners[lax.div(k, 6), target * 6 + lax.rem(k, 6)]
        d = lax.div(slot, 4)
        return lax.rem(slot, 4), pieces[lax.div(d, 8), lax.rem(lax.div(d, 2), 4), lax.rem(d, 2)]

    def fill(o, start, arrived=None):
        @pl.loop(0, 6)
        def _(n):
            where, rows = wanted(plane[o], start + n)
            if arrived is not None:
                rows = lax.select(where == t, rows, arrived[n])
            hold[o - 1, start + n] = rows

    @step((ZF,))
    def _():
        roots.finish()
        fill(2, 0)
        fill(2, 6)
        kept["z", 0] = [
            net.start(hold.at[1, first_k], far_in.at[0], right),
            net.start(hold.at[1, last_k], far_in.at[1], left),
        ]

    @step((ZP,))
    def _():
        fill(1, 6)
        fill(3, 0)
        kept["z", 1] = [
            net.start(hold.at[0, last_k], plain_in.at[0], right),
            net.start(hold.at[2, first_k], plain_in.at[1], left),
        ]

    @step((ZM, 0))
    def _():
        kept["z", 0][0].wait_recv()
        fill(1, 0, far_in.at[0])
        kept["z", 2] = net.start(hold.at[0, first_k], merged_in.at[0], right)

    @step((ZM, 1))
    def _():
        kept["z", 0][1].wait_recv()
        fill(3, 6, far_in.at[1])
        kept["z", 3] = net.start(hold.at[2, last_k], merged_in.at[1], left)

    root_send, root_mid = v["root_send"], v["root_mid"]

    @step((ZSEL,))
    def _():
        for copy in kept["z", 1] + [kept["z", 2], kept["z", 3]]:
            copy.wait_recv()
        for side in range(2):
            for block in range(6):
                where, rows = wanted(t, side * 6 + block)
                away = wrap(where - t)
                if side == 0:
                    other_rows = lax.select(away == 1, plain_in[1, block], merged_in[0, block])
                else:
                    other_rows = lax.select(away == 3, plain_in[0, block], merged_in[1, block])
                rows = lax.select(away == 0, rows, other_rows)
                for s in range(2):
                    line, rank = spot(s, block)
                    root_send[s, line, side, rank] = rows[s]

    g_send, g_mid = v["g_send"], v["g_mid"]

    def sum_up(s):
        sums.finish(s, g)
        here, there = g.at[:, s], every[s].at[t]
        kept["g", s] = [net.start(here, there, right), net.start(here, there, left)]
        kept["g_own", s] = net.local(here, there)

    def pass_along(s, way):
        kept["g", s][way].wait_recv()
        rows = every[s].at[plane[3], lo] if way == 0 else every[s].at[plane[1], hi]
        kept["g_pass", s, way] = net.start(rows, rows, right if way == 0 else left)

    def send_g(s):
        for block in range(6):
            line, rank = spot(s, block)
            g_send[s, line, 0, rank] = g[block, s]
        kept["gl", s] = WorkerLeg(net, s, g_send.at[s], g_mid.at[s], v["g_relay"].at[s])

    def send_roots(s):
        kept["rl", s] = WorkerLeg(net, s, root_send.at[s], root_mid.at[s], v["r_relay"].at[s])

    mats = v["mats"]

    def gather(name, leg, s, mid, first, count, relay):
        def land(j, h):
            if s == 0:
                return mats.at[pl.ds(first, count), half(h), j, c, 0]
            return mats.at[pl.ds(first, count), j, half(h), c, 1]

        kept[leg, s].finish()
        kept[name, s] = Gather(workers, s, lambda rank, h: mid.at[s, :, half(h), rank], land, relay.at[s])

    shares = [net.make(mats.at[m, :, :, c], mats.at[m, :, :, c], net.pair) for m in (2, 1)]
    net.open += [(copy, workers.is_worker) for copy in shares]
    mixed, result = v["mixed"], v["result"]

    def share(name, k):
        @pl.when(workers.is_worker)
        def _():
            for s in range(2):
                kept[name, s].wait_here()
            shares[k].start()

    def column_tiles(function):
        @pl.loop(0, 4)
        def _(n):
            function(pl.ds(pl.multiple_of(n * 256, 256), 256))

    @step((MMA,))
    def _():
        @pl.when(workers.is_worker)
        def _():
            shares[0].wait_recv()

            @column_tiles
            def _(cols):
                block = mats[2, :, :, :, :, :, cols].reshape(1024, 256)
                rows = mats[0, :, :, c].reshape(512, 1024)
                mixed[:, cols] = jnp.dot(rows, block, preferred_element_type=f32).astype(bf16)

    @step((MMB,))
    def _():
        @pl.when(workers.is_worker)
        def _():
            shares[1].wait_recv()

            @column_tiles
            def _(cols):
                block = mats[1, :, :, :, :, :, cols].reshape(1024, 256)
                rows = jnp.dot(mixed[...], block, preferred_element_type=f32).astype(bf16)
                result[:, :, :, :, cols] = rows.reshape(4, 4, 2, 16, 256)

    back, home = v["back"], v["home"]

    @step((SP,))
    def _():
        for s in range(2):
            kept["sp", s] = Spread(
                workers,
                s,
                lambda j, h, s=s: result.at[half(h), j, 0] if s == 0 else result.at[j, half(h), 1],
                lambda rank, h, s=s: back.at[s, rank, half(h)],
                v["u_relay"].at[s],
            )

    def go_home(s):
        kept["sp", s].finish()
        kept["ul", s] = HomeLeg(net, s, back.at[s], home.at[s], v["u_relay2"].at[s])

    @step((ULE,))
    def _():
        for s in range(2):
            kept["ul", s].finish()
            for block in range(6):
                line, rank = spot(s, block)
                v["update"][block, s] = home[s, line, rank]

    steps[(OWE,)] = owned.finish
    steps[(SH0,)] = functools.partial(share, "gg", 0)
    steps[(SH1,)] = functools.partial(share, "rg", 1)
    for s in range(2):
        bind = functools.partial
        steps[RO1, s] = bind(roots.first, s)
        steps[RO2, s] = bind(roots.second, s)
        steps[OW1, s] = bind(pack_owned, s)
        steps[OW2, s] = bind(owned.second, s)
        steps[FAR, s] = bind(sums.far, s)
        steps[SEC, s] = bind(sums.second, s)
        steps[G, s] = bind(sum_up, s)
        steps[GL, s] = bind(send_g, s)
        steps[RL, s] = bind(send_roots, s)
        steps[GG, s] = bind(gather, "gg", "gl", s, g_mid, 2, 1, v["g_relay2"])
        steps[RG, s] = bind(gather, "rg", "rl", s, root_mid, 0, 2, v["r_relay2"])
        steps[GGF, s] = lambda s=s: kept["gg", s].forward()
        steps[RGF, s] = lambda s=s: kept["rg", s].forward()
        steps[SPF, s] = lambda s=s: kept["sp", s].forward()
        steps[UL, s] = bind(go_home, s)
        for way in range(2):
            steps[PLAIN, way, s] = bind(sums.plain, way, s)
            steps[MERGED, way, s] = bind(sums.merged, way, s)
            steps[SECP, way, s] = bind(sums.second_plain, way, s)
            steps[SECM, way, s] = bind(sums.second_merged, way, s)
            steps[ZAF, s, way] = bind(pass_along, s, way)
            for name, trip, leg in ((RO1F, roots, 0), (RO2F, roots, 1), (OW1F, owned, 0), (OW2F, owned, 1)):
                steps[name, s, way] = (
                    lambda trip=trip, leg=leg, s=s, way=way: trip.legs[leg, s].forward(way)
                )
            for name, leg in ((GLF, "gl"), (RLF, "rl"), (ULF, "ul")):
                steps[name, s, way] = lambda leg=leg, s=s, way=way: kept[leg, s].forward(way)
    assert sorted(steps) == sorted(ORDER)
    for name in ORDER:
        steps[name]()
    net.close()


def step(grads, owner_slots, root):
    tile = (16, root.shape[1])
    vmem = {
        "own": (2, 4, 6, 4),
        "cin": (2, 4, 6, 4),
        "first_in": (3, 2, 2, 3, 4),
        "f": (2, 4, 6),
        "second_in": (3, 2, 2, 3),
        "g": (6, 2),
        "every_0": (4, 6),
        "every_1": (4, 6),
        "root_middle": (2, 4, 4, 2),
        "root_relay": (2, 2, 2, 2, 2),
        "roots": (4, 4, 2, 2),
        "g_send": (2, 4, 1, 2),
        "g_mid": (2, 1, 4, 2),
        "g_relay2": (2, 2, 1, 2),
        "mats": (3, 4, 4, 2, 2),
        "owned_parcels": (2, 4, 4, 2),
        "owned_middle": (2, 4, 4, 2),
        "owned_relay": (2, 2, 2, 2, 2),
        "hold": (3, 12, 2),
        "z_far": (2, 6, 2),
        "z_plain": (2, 6, 2),
        "z_merged": (2, 6, 2),
        "root_send": (2, 4, 2, 2),
        "root_mid": (2, 2, 4, 2),
        "r_relay2": (2, 2, 2, 2),
        "result": (4, 4, 2),
        "back": (2, 2, 4),
        "home": (2, 4, 2),
        "u_relay": (2, 2, 2),
    }
    scratch = {name: pltpu.VMEM(shape + tile, bf16) for name, shape in vmem.items()}
    scratch["g_relay"] = pltpu.VMEM((2, 2, 1, 2, 16, tile[1] // 2), bf16)
    scratch["r_relay"] = pltpu.VMEM((2, 2, 2, 2, 16, tile[1] // 2), bf16)
    scratch["u_relay2"] = pltpu.VMEM((2, 2, 2, 16, tile[1] // 2), bf16)
    scratch["mixed"] = pltpu.VMEM((512, tile[1]), bf16)
    scratch["blocks"] = pltpu.SMEM((32,), jnp.int32)
    scratch["send"] = pltpu.SemaphoreType.DMA((288,))
    scratch["recv"] = pltpu.SemaphoreType.DMA((288,))
    names = ["parts", "owners", "root", "owned", "update"] + list(scratch)
    in_vmem = pl.BlockSpec(memory_space=pltpu.VMEM)
    anywhere = pl.BlockSpec(memory_space=pl.ANY)
    owned, update = pl.pallas_call(
        functools.partial(step_kernel, names),
        out_shape=(
            jax.ShapeDtypeStruct((4, 4, 2, 2) + tile, bf16),
            jax.ShapeDtypeStruct((6, 2) + tile, bf16),
        ),
        in_specs=[anywhere, pl.BlockSpec(memory_space=pltpu.SMEM), anywhere],
        out_specs=(anywhere, in_vmem),
        scratch_shapes=list(scratch.values()),
        compiler_params=pltpu.CompilerParams(
            collective_id=0, has_side_effects=True, vmem_limit_bytes=62 * 2**20
        ),
    )(grads.reshape((6, 4, 4, 2, 2) + tile), owner_slots, root.reshape((4, 4, 2, 2) + tile))
    return owned.reshape(1024, tile[1]), update.reshape(6, 32, tile[1])


def stats_kernel(owners, block_ref, old_ref, update, new_ref, update_out, block, turned, stats, held, sem):
    me = lax.axis_index("dp") * 4 + lax.axis_index("tensor")
    parts = [pl.ds(256 * i, 256) for i in range(4)]
    copy = pltpu.make_async_copy
    fetches = [copy(block_ref.at[parts[i]], block.at[parts[i]], sem.at[i]) for i in range(4)]
    loads = [copy(old_ref.at[parts[i]], stats.at[parts[i]], sem.at[4 + i]) for i in range(4)]
    stores = [copy(stats.at[parts[i]], new_ref.at[parts[i]], sem.at[8 + i]) for i in range(4)]
    take, give = copy(update, held, sem.at[12]), copy(held, update_out, sem.at[13])
    for each in fetches + [take] + loads:
        each.start()
    is_left, is_right = owners[0, 0] == me, owners[1, 0] == me
    for b in range(1, 24):
        is_left = jnp.logical_or(is_left, owners[0, b] == me)
        is_right = jnp.logical_or(is_right, owners[1, b] == me)
    named = jnp.logical_or(is_left, is_right)

    def turn(part):
        turned[:, part] = block[part, :].T

    for i in range(4):
        fetches[i].wait()
        pl.when(named)(functools.partial(turn, parts[i]))
    take.wait()
    give.start()

    def blend(part, rows, other):
        gram = jnp.dot(rows[part, :], other[...], preferred_element_type=f32)
        stats[part, :] = decay_rate * stats[part, :] + (1 - decay_rate) * (gram * block.shape[1] ** (-0.5))

    for i in range(4):
        loads[i].wait()
        pl.when(is_left)(functools.partial(blend, parts[i], block, turned))
        pl.when(is_right)(functools.partial(blend, parts[i], turned, block))
        stores[i].start()
    for each in stores + [give]:
        each.wait()


def finish_stats(owner_slots, block, old, update):
    anywhere = pl.BlockSpec(memory_space=pl.ANY)
    return pl.pallas_call(
        stats_kernel,
        out_shape=(
            jax.ShapeDtypeStruct(old.shape, f32),
            jax.ShapeDtypeStruct(update.shape, bf16),
        ),
        in_specs=[pl.BlockSpec(memory_space=pltpu.SMEM), anywhere, anywhere, anywhere],
        out_specs=(anywhere, anywhere),
        scratch_shapes=[
            pltpu.VMEM(block.shape, bf16),
            pltpu.VMEM(block.shape, bf16),
            pltpu.VMEM(old.shape, f32),
            pltpu.VMEM(update.shape, bf16),
            pltpu.SemaphoreType.DMA((14,)),
        ],
        compiler_params=pltpu.CompilerParams(vmem_limit_bytes=60 * 2**20),
    )(owner_slots, block, old, update)


def body(partial_grads, owner_slots, statistics, inv_roots):
    owners = owner_slots.T
    owned, update = step(partial_grads[0], owners, inv_roots[0, 0, 0])
    new_stats, update = finish_stats(owners, owned, statistics[0, 0, 0], update)
    return (new_stats[None, None, None], update)


def solution(mesh):
    return jax.shard_map(
        body,
        mesh=mesh,
        in_specs=(
            P("dp", "tensor", None, None),
            P(),
            P("dp", "tensor", None, None, None),
            P("dp", "tensor", None, None, None),
        ),
        out_specs=(P("dp", "tensor", None, None, None), P("tensor", "dp", None)),
        check_vma=False,
    )
```

time: 546 us -> 134 us (0.25)
  blocking collectives: 267 us -> 0 us
  waiting for transfers between devices: 191 us -> 0 us
  Pallas kernels: 0 us -> 133 us
  local copies, waits for them, and re-layouts: 31.2 us -> 0 us
  matrix products: 29.4 us -> 0 us
  between operations: 15.8 us -> 0.64 us
  starting transfers between devices: 5.96 us -> 0 us
    all_to_all x4 -> x0, blocking collectives: 267 us -> none  [the longest x1 102 us: body(): lax.all_to_all(outgoing, 'dp', split_axis=1, concat_axis=1, tiled=True)]
    pallas_call x0 -> x2, Pallas kernels: none -> 133 us  [the longest x1 126 us: step(): pl.pallas_call(functools.partial(step_kernel, names), out_shape=(jax.Shap...]
    reduce_scatter x2 -> x0, waiting for transfers between devices: 116 us -> none  [the longest x1 110 us: body(): lax.psum_scatter(grad_parts.astype(jnp.float32).astype(jnp.bfloat16), 'dp...]
    psum x1 -> x0, waiting for transfers between devices: 46.2 us -> none  [body(): mixed_all = lax.psum(mixed_part.astype(jnp.bfloat16), 'tensor')]
    dot_general x7 -> x0, matrix products: 29.4 us -> none  [the longest x1 8.05 us: body(): jnp.einsum('cxk,cyk->cxy', turned, turned, preferred_element_type=jnp.flo...]
    all_to_all x1 -> x0, waiting for transfers between devices: 28.2 us -> none  [body(): lax.all_to_all(mixed.reshape(capacity, n_data, row_piece, block_width), '...]
    convert_element_type x3 -> x0, local copies, waits for them, and re-layouts: 14.5 us -> none  [the longest x1 11.3 us: body(): outgoing = jnp.einsum('dtci,iry->cdtry', group_cols, summed, preferred_el...]
    all_to_all x1 -> x0, local copies, waits for them, and re-layouts: 11.4 us -> none  [body(): lax.all_to_all(outgoing, 'dp', split_axis=1, concat_axis=1, tiled=True)]
  transfers between devices with their start and end apart: 4 -> 0, of which waited for: 4 -> 0; matrix products, arithmetic and copies ran while one was open for 2% -> 0% of each run, Pallas kernels for 0% -> 0%
where the time goes in v1:
time: 134 us
  Pallas kernels  133 us (99%)
    pallas_call x1, Pallas kernels, step(): pl.pallas_call(functools.partial(step_kernel, names), out_shape=(jax.Shap...  126 us
    pallas_call x1, Pallas kernels, finish_stats(): pl.pallas_call(stats_kernel, out_shape=(jax.ShapeDtypeStruct(old.shape, f...  6.75 us

profile of v1, /device:TPU:1, one launch (start us, length us, event | category | flops | bytes accessed | tf_op | source)
XLA Modules:
  0.0 133.7 jit_solution(8379957263559933899)
XLA Ops:
  0.6 126.3 %shard_map.59 = (bf16[4,4,2,2,16,1024]{5,4,3,2,1,0:T(8,128)(2,1)}, bf16[6,2,16,1024]{3,2,1,0:T(8,128)(2,1)}) custom-call(bf16[6,4,4,2,2,16,1024]{6,5,4,3,2,1,0:T(8,128)(2,1)} %bitcast.7, s32[2,24]{1,0:T(2,128)} %bitcast.12, bf16[4,4,2,2,16,1024]{5,4,3,2,1,0:T(8,128)(2,1)} %bitcast.10), custom_call_target="tpu_custom_call" | custom-call | tf_op jit(solution)/shard_map/pallas_call | solution.py:856
  127.0 6.7 %shard_map.60 = (f32[1024,1024]{1,0:T(8,128)}, bf16[6,32,1024]{2,1,0:T(8,128)(2,1)}) custom-call(s32[2,24]{1,0:T(2,128)} %bitcast.13, bf16[1024,1024]{1,0:T(8,128)(2,1)} %bitcast.9, f32[1024,1024]{1,0:T(8,128)} %bitcast.8, bf16[6,32,1024]{2,1,0:T(8,128)(2,1)} %bitcast.11), custom_call_target="tpu_custom_call" | custom-call | tf_op jit(solution)/shard_map/pallas_call | solution.py:912

commit v2 on v1

--- a/solution.py
+++ b/solution.py
@@ -68,12 +68,13 @@
         copy.start()
         return copy
 
-    def close(self):
-        for copy, when in self.open:
+    def close(self, count):
+        for copy, when in self.open[:count]:
             if when is None:
                 copy.wait_send()
             else:
                 pl.when(when)(copy.wait_send)
+        self.open = self.open[count:]
 
 
 class Exchange:
@@ -536,6 +537,8 @@
     BLK, FAR, FETCH, G, GG, GGF, GL, GLF, MERGED, MMA, MMB, OW1, OW1F, OW2, OW2F, OWE, PLAIN, RG, RGF, RL, RLF,
     RO1, RO1F, RO2, RO2F, SEC, SECM, SECP, SH0, SH1, SP, SPF, UL, ULE, ULF, ZAF, ZF, ZM, ZP, ZSEL,
 ) = range(40)
+CLOSING = (ULF, 0, 1)
+RESULTS = 40
 ORDER = (
     (RO1, 1), (RO1, 0), (BLK,), (RO1F, 1, 1), (RO1F, 0, 1), (RO1F, 1, 0), (RO1F, 0, 0), (FETCH,), (RO2, 1),
     (RO2, 0), (RO2F, 0, 0), (RO2F, 1, 1), (RO2F, 1, 0), (FAR, 0), (PLAIN, 0, 0), (RO2F, 0, 1), (FAR, 1), (ZF,),
@@ -589,7 +592,7 @@
     )
     parcels = v["owned_parcels"]
     owned = PlaneExchange(
-        net, lambda s, x, y: parcels.at[s, x, y], v["owned_middle"], v["owned"], v["owned_relay"]
+        net, lambda s, x, y: parcels.at[s, x, y], v["owned_middle"], v["results"].at[pl.ds(0, 4)], v["owned_relay"]
     )
 
     def pack_owned(s):
@@ -769,7 +772,8 @@
             kept["ul", s].finish()
             for block in range(6):
                 line, rank = spot(s, block)
-                v["update"][block, s] = home[s, line, rank]
+                v["update"][block // 2, block % 2, s] = home[s, line, rank]
+        kept["update"] = net.local(v["update"], v["results"].at[4, pl.ds(0, 3)])
 
     steps[(OWE,)] = owned.finish
     steps[(SH0,)] = functools.partial(share, "gg", 0)
@@ -805,8 +809,13 @@
                 steps[name, s, way] = lambda leg=leg, s=s, way=way: kept[leg, s].forward(way)
     assert sorted(steps) == sorted(ORDER)
     for name in ORDER:
+        if name == (MMA,):
+            early = len(net.open)
+        if name == CLOSING:
+            net.close(early)
         steps[name]()
-    net.close()
+    kept["update"].wait()
+    net.close(len(net.open))
 
 
 def step(grads, owner_slots, root):
@@ -840,6 +849,7 @@
         "result": (4, 4, 2),
         "back": (2, 2, 4),
         "home": (2, 4, 2),
+        "update": (3, 2, 2),
         "u_relay": (2, 2, 2),
     }
     scratch = {name: pltpu.VMEM(shape + tile, bf16) for name, shape in vmem.items()}
@@ -848,35 +858,30 @@
     scratch["u_relay2"] = pltpu.VMEM((2, 2, 2, 16, tile[1] // 2), bf16)
     scratch["mixed"] = pltpu.VMEM((512, tile[1]), bf16)
     scratch["blocks"] = pltpu.SMEM((32,), jnp.int32)
-    scratch["send"] = pltpu.SemaphoreType.DMA((288,))
-    scratch["recv"] = pltpu.SemaphoreType.DMA((288,))
-    names = ["parts", "owners", "root", "owned", "update"] + list(scratch)
-    in_vmem = pl.BlockSpec(memory_space=pltpu.VMEM)
+    scratch["send"] = pltpu.SemaphoreType.DMA((256,))
+    scratch["recv"] = pltpu.SemaphoreType.DMA((256,))
+    names = ["parts", "owners", "root", "results"] + list(scratch)
     anywhere = pl.BlockSpec(memory_space=pl.ANY)
-    owned, update = pl.pallas_call(
+    return pl.pallas_call(
         functools.partial(step_kernel, names),
-        out_shape=(
-            jax.ShapeDtypeStruct((4, 4, 2, 2) + tile, bf16),
-            jax.ShapeDtypeStruct((6, 2) + tile, bf16),
-        ),
+        out_shape=jax.ShapeDtypeStruct((RESULTS, 4, 2, 2) + tile, bf16),
         in_specs=[anywhere, pl.BlockSpec(memory_space=pltpu.SMEM), anywhere],
-        out_specs=(anywhere, in_vmem),
+        out_specs=anywhere,
         scratch_shapes=list(scratch.values()),
         compiler_params=pltpu.CompilerParams(
-            collective_id=0, has_side_effects=True, vmem_limit_bytes=62 * 2**20
+            collective_id=0, has_side_effects=True, vmem_limit_bytes=58 * 2**20
         ),
     )(grads.reshape((6, 4, 4, 2, 2) + tile), owner_slots, root.reshape((4, 4, 2, 2) + tile))
-    return owned.reshape(1024, tile[1]), update.reshape(6, 32, tile[1])
-
-
-def stats_kernel(owners, block_ref, old_ref, update, new_ref, update_out, block, turned, stats, held, sem):
+
+
+def stats_kernel(owners, results, old_ref, new_ref, update_out, block, turned, stats, held, sem):
     me = lax.axis_index("dp") * 4 + lax.axis_index("tensor")
     parts = [pl.ds(256 * i, 256) for i in range(4)]
     copy = pltpu.make_async_copy
-    fetches = [copy(block_ref.at[parts[i]], block.at[parts[i]], sem.at[i]) for i in range(4)]
+    fetches = [copy(results.at[i], block.at[i], sem.at[i]) for i in range(4)]
     loads = [copy(old_ref.at[parts[i]], stats.at[parts[i]], sem.at[4 + i]) for i in range(4)]
     stores = [copy(stats.at[parts[i]], new_ref.at[parts[i]], sem.at[8 + i]) for i in range(4)]
-    take, give = copy(update, held, sem.at[12]), copy(held, update_out, sem.at[13])
+    take, give = copy(results.at[4, pl.ds(0, 3)], held, sem.at[12]), copy(held, update_out, sem.at[13])
     for each in fetches + [take] + loads:
         each.start()
     is_left, is_right = owners[0, 0] == me, owners[1, 0] == me
@@ -885,54 +890,58 @@
         is_right = jnp.logical_or(is_right, owners[1, b] == me)
     named = jnp.logical_or(is_left, is_right)
 
-    def turn(part):
-        turned[:, part] = block[part, :].T
+    def rows(i):
+        return block[i].reshape(256, 1024)
+
+    def turn(i):
+        turned[:, parts[i]] = rows(i).T
 
     for i in range(4):
         fetches[i].wait()
-        pl.when(named)(functools.partial(turn, parts[i]))
+        pl.when(named)(functools.partial(turn, i))
     take.wait()
     give.start()
 
-    def blend(part, rows, other):
-        gram = jnp.dot(rows[part, :], other[...], preferred_element_type=f32)
-        stats[part, :] = decay_rate * stats[part, :] + (1 - decay_rate) * (gram * block.shape[1] ** (-0.5))
+    def blend(i, some, other):
+        gram = jnp.dot(some, other, preferred_element_type=f32)
+        stats[parts[i], :] = decay_rate * stats[parts[i], :] + (1 - decay_rate) * (gram * 1024 ** (-0.5))
 
     for i in range(4):
         loads[i].wait()
-        pl.when(is_left)(functools.partial(blend, parts[i], block, turned))
-        pl.when(is_right)(functools.partial(blend, parts[i], turned, block))
+        pl.when(is_left)(lambda i=i: blend(i, rows(i), turned[...]))
+        pl.when(is_right)(lambda i=i: blend(i, turned[parts[i], :], block[...].reshape(1024, 1024)))
         stores[i].start()
     for each in stores + [give]:
         each.wait()
 
 
-def finish_stats(owner_slots, block, old, update):
+def finish_stats(owner_slots, results, old):
     anywhere = pl.BlockSpec(memory_space=pl.ANY)
+    tile = results.shape[-2:]
     return pl.pallas_call(
         stats_kernel,
         out_shape=(
             jax.ShapeDtypeStruct(old.shape, f32),
-            jax.ShapeDtypeStruct(update.shape, bf16),
+            jax.ShapeDtypeStruct((3, 2, 2) + tile, bf16),
         ),
-        in_specs=[pl.BlockSpec(memory_space=pltpu.SMEM), anywhere, anywhere, anywhere],
+        in_specs=[pl.BlockSpec(memory_space=pltpu.SMEM), anywhere, anywhere],
         out_specs=(anywhere, anywhere),
         scratch_shapes=[
-            pltpu.VMEM(block.shape, bf16),
-            pltpu.VMEM(block.shape, bf16),
+            pltpu.VMEM((4, 4, 2, 2) + tile, bf16),
+            pltpu.VMEM((1024, 1024), bf16),
             pltpu.VMEM(old.shape, f32),
-            pltpu.VMEM(update.shape, bf16),
+            pltpu.VMEM((3, 2, 2) + tile, bf16),
             pltpu.SemaphoreType.DMA((14,)),
         ],
-        compiler_params=pltpu.CompilerParams(vmem_limit_bytes=60 * 2**20),
-    )(owner_slots, block, old, update)
+        compiler_params=pltpu.CompilerParams(vmem_limit_bytes=40 * 2**20),
+    )(owner_slots, results, old)
 
 
 def body(partial_grads, owner_slots, statistics, inv_roots):
     owners = owner_slots.T
-    owned, update = step(partial_grads[0], owners, inv_roots[0, 0, 0])
-    new_stats, update = finish_stats(owners, owned, statistics[0, 0, 0], update)
-    return (new_stats[None, None, None], update)
+    results = step(partial_grads[0], owners, inv_roots[0, 0, 0])
+    new_stats, update = finish_stats(owners, results, statistics[0, 0, 0])
+    return (new_stats[None, None, None], update.reshape(6, 32, 1024))
 
 
 def solution(mesh):

time: 134 us -> 131 us (0.978)
  Pallas kernels: 133 us -> 129 us
    pallas_call x1, Pallas kernels: 6.75 us -> 4.43 us  [finish_stats(): pl.pallas_call(stats_kernel, out_shape=(jax.ShapeDtypeStruct(old.shape, f...]
    pallas_call x1, Pallas kernels: 126 us -> 125 us  [step(): pl.pallas_call(functools.partial(step_kernel, names), out_shape=jax.Shape...]
where the time goes in v2:
time: 131 us; the launch traced here: 130 us
  Pallas kernels  129 us (98%)
    pallas_call x1, Pallas kernels, step(): pl.pallas_call(functools.partial(step_kernel, names), out_shape=jax.Shape...  125 us
    pallas_call x1, Pallas kernels, finish_stats(): pl.pallas_call(stats_kernel, out_shape=(jax.ShapeDtypeStruct(old.shape, f...  4.43 us

profile of v2, /device:TPU:1, one launch (start us, length us, event | category | flops | bytes accessed | tf_op | source)
XLA Modules:
  0.0 130.0 jit_solution(10171116681612659757)
XLA Ops:
  0.6 0.0 copy-start
  0.6 0.0 copy-start.1
  0.7 124.9 %shard_map.59.results = bf16[40,4,2,2,16,1024]{5,4,3,2,1,0:T(8,128)(2,1)} custom-call(bf16[6,4,4,2,2,16,1024]{6,5,4,3,2,1,0:T(8,128)(2,1)} %bitcast.9, s32[2,24]{1,0:T(2,128)} %bitcast.7, bf16[4,4,2,2,16,1024]{5,4,3,2,1,0:T(8,128)(2,1)} %bitcast.10), custom_call_target="tpu_custom_call" | custom-call | tf_op jit(solution)/shard_map/pallas_call | solution.py:865
  125.6 0.0 copy-done
  125.6 0.0 copy-done.1
  125.6 4.4 %shard_map.60 = (f32[1024,1024]{1,0:T(8,128)}, bf16[3,2,2,16,1024]{4,3,2,1,0:T(8,128)(2,1)}) custom-call(s32[2,24]{1,0:T(2,128)S(1)} %bitcast.8, bf16[40,4,2,2,16,1024]{5,4,3,2,1,0:T(8,128)(2,1)} %shard_map.59.results, f32[1024,1024]{1,0:T(8,128)S(1)} %bitcast.6), custom_call_target="tpu_custom_call" | custom-call | tf_op jit(solution)/shard_map/pallas_call | solution.py:921
Async XLA Ops:
  0.6 124.9 %copy-start = (f32[1,1,1,1024,1024]{4,3,2,1,0:T(8,128)S(1)}, f32[1,1,1,1024,1024]{4,3,2,1,0:T(8,128)}, u32[]{:S(2)}) copy-start(f32[1,1,1,1024,1024]{4,3,2,1,0:T(8,128)} %param.6) | copy-start | bytes 12582916
  0.6 124.9 %copy-start.1 = (s32[24,2]{0,1:T(2,128)S(1)}, s32[24,2]{0,1:T(2,128)}, u32[]{:S(2)}) copy-start(s32[24,2]{0,1:T(2,128)} %param.5) | copy-start | bytes 580

commit v3 on v2

--- a/solution.py
+++ b/solution.py
@@ -61,6 +61,17 @@
             pl.when(when)(copy.start)
         self.open.append((copy, when))
         return copy
+
+    def fork(self, two, ends, device):
+        copies = []
+        for count, when in ((2, two), (1, jnp.logical_not(two))):
+            src, dst = ends(pl.ds(0, count))
+            copies.append(self.start(src, dst, device, when))
+        return copies
+
+    def join(self, two, copies):
+        pl.when(two)(copies[0].wait_recv)
+        pl.when(jnp.logical_not(two))(copies[1].wait_recv)
 
     def local(self, src, dst):
         copy = pltpu.make_async_copy(src, dst, self.send.at[self.count])
@@ -180,69 +191,48 @@
 
 class WorkerLeg:
     def __init__(self, net, s, source, target, relay):
-        self.net, self.s, self.axis = net, s, "xy"[s]
+        self.net, self.axis, self.target, self.relay = net, "xy"[s], target, relay
         here = net.at[self.axis]
-        self.target, self.relay = target, relay
         self.i = i = [wrap(here + o) for o in range(4)]
         self.two = [v < 2 if s == 0 else v >= 2 for v in i]
         wide = relay.shape[-1]
         self.cols = [pl.ds(0, wide), pl.ds(wide, wide)]
-
-        def when(o, rank):
-            return self.two[o] if rank else None
-
-        self.when = when
         self.far = [
-            [
-                net.start(
-                    source.at[i[2], :, rank, :, self.cols[way]],
-                    relay.at[way, :, rank],
-                    net.near(self.axis, 1 - 2 * way),
-                    when(2, rank),
-                )
-                for way in range(2)
-            ]
-            for rank in range(2)
-        ]
-        self.direct = [
-            [
-                net.start(
-                    source.at[i[o], :, rank], target.at[:, i[0], rank], net.near(self.axis, step), when(o, rank)
-                )
-                for o, step in ((1, 1), (3, -1))
-            ]
-            for rank in range(2)
+            net.fork(
+                self.two[2],
+                lambda ranks: (source.at[i[2], :, ranks, :, self.cols[way]], relay.at[way, :, ranks]),
+                net.near(self.axis, 1 - 2 * way),
+            )
+            for way in range(2)
+        ]
+        self.arrive = [
+            net.fork(
+                self.two[o],
+                lambda ranks: (source.at[i[o], :, ranks], target.at[:, i[0], ranks]),
+                net.near(self.axis, step),
+            )
+            for o, step in ((1, 1), (3, -1))
         ]
         self.own = net.local(source.at[i[0]], target.at[:, i[0]])
-        self.passed = [[], []]
 
     def forward(self, way):
         o, goal = ((3, 1), (1, 3))[way]
-        for rank in range(2):
-            arrived = self.far[rank][way]
-            when = self.when(goal, rank)
-            if when is None:
-                arrived.wait_recv()
-            else:
-                pl.when(when)(arrived.wait_recv)
-            self.passed[rank].append(
-                self.net.start(
-                    self.relay.at[way, :, rank],
-                    self.target.at[:, self.i[o], rank, :, self.cols[way]],
-                    self.net.near(self.axis, 1 - 2 * way),
-                    when,
-                )
+        self.net.join(self.two[goal], self.far[way])
+        self.arrive.append(
+            self.net.fork(
+                self.two[goal],
+                lambda ranks: (
+                    self.relay.at[way, :, ranks],
+                    self.target.at[:, self.i[o], ranks, :, self.cols[way]],
+                ),
+                self.net.near(self.axis, 1 - 2 * way),
             )
+        )
 
     def finish(self):
         self.own.wait()
-        for copy in self.direct[0] + self.passed[0]:
-            copy.wait_recv()
-
-        @pl.when(self.two[0])
-        def _():
-            for copy in self.direct[1] + self.passed[1]:
-                copy.wait_recv()
+        for copies in self.arrive:
+            self.net.join(self.two[0], copies)
 
 
 class HomeLeg:
@@ -254,54 +244,42 @@
         wide = relay.shape[-1]
         self.cols = [pl.ds(0, wide), pl.ds(wide, wide)]
         self.far = [
-            [
-                net.start(
-                    back.at[rank, i[2], :, self.cols[way]],
-                    relay.at[way, rank],
-                    net.near(self.axis, 1 - 2 * way),
-                    self.when(0, rank),
-                )
-                for way in range(2)
-            ]
-            for rank in range(2)
+            net.fork(
+                self.two[0],
+                lambda ranks: (back.at[ranks, i[2], :, self.cols[way]], relay.at[way, ranks]),
+                net.near(self.axis, 1 - 2 * way),
+            )
+            for way in range(2)
         ]
         self.direct = [
-            [
-                net.start(back.at[rank, i[o]], home.at[i[0], rank], net.near(self.axis, step), self.when(0, rank))
-                for o, step in ((1, 1), (3, -1))
-            ]
-            for rank in range(2)
+            net.fork(
+                self.two[0],
+                lambda ranks: (back.at[ranks, i[o]], home.at[i[0], ranks]),
+                net.near(self.axis, step),
+            )
+            for o, step in ((1, 1), (3, -1))
         ]
         self.own = net.local(back.at[:, i[0]], home.at[i[0]])
-        self.passed = [[], []]
-
-    def when(self, o, rank):
-        return self.two[o] if rank else None
-
-    def arrived(self, copy, o, rank):
-        if rank:
-            pl.when(self.two[o])(copy.wait_recv)
-        else:
-            copy.wait_recv()
+        self.passed = []
 
     def forward(self, way):
         o = (3, 1)[way]
-        for rank in range(2):
-            self.arrived(self.far[rank][way], o, rank)
-            self.passed[rank].append(
-                self.net.start(
-                    self.relay.at[way, rank],
-                    self.home.at[self.i[o], rank, :, self.cols[way]],
-                    self.net.near(self.axis, 1 - 2 * way),
-                    self.when(o, rank),
-                )
+        self.net.join(self.two[o], self.far[way])
+        self.passed.append(
+            self.net.fork(
+                self.two[o],
+                lambda ranks: (
+                    self.relay.at[way, ranks],
+                    self.home.at[self.i[o], ranks, :, self.cols[way]],
+                ),
+                self.net.near(self.axis, 1 - 2 * way),
             )
+        )
 
     def finish(self):
         self.own.wait()
-        for rank in range(2):
-            for copy, o in zip(self.direct[rank] + self.passed[rank], (3, 1, 2, 2)):
-                self.arrived(copy, o, rank)
+        for copies, o in zip(self.direct + self.passed, (3, 1, 2, 2)):
+            self.net.join(self.two[o], copies)
 
 
 def spot(s, block):

time: 131 us -> 132 us (level)
  no operation moved by 1% of the time
where the time goes in v3:
time: 132 us; the launch traced here: 130 us
  Pallas kernels  129 us (98%)
    pallas_call x1, Pallas kernels, step(): pl.pallas_call(functools.partial(step_kernel, names), out_shape=jax.Shape...  125 us
    pallas_call x1, Pallas kernels, finish_stats(): pl.pallas_call(stats_kernel, out_shape=(jax.ShapeDtypeStruct(old.shape, f...  4.43 us

profile of v3, /device:TPU:1, one launch (start us, length us, event | category | flops | bytes accessed | tf_op | source)
XLA Modules:
  0.0 130.0 jit_solution(6622909125434496846)
XLA Ops:
  0.6 0.0 copy-start
  0.6 0.0 copy-start.1
  0.7 124.9 %shard_map.59.results = bf16[40,4,2,2,16,1024]{5,4,3,2,1,0:T(8,128)(2,1)} custom-call(bf16[6,4,4,2,2,16,1024]{6,5,4,3,2,1,0:T(8,128)(2,1)} %bitcast.9, s32[2,24]{1,0:T(2,128)} %bitcast.7, bf16[4,4,2,2,16,1024]{5,4,3,2,1,0:T(8,128)(2,1)} %bitcast.10), custom_call_target="tpu_custom_call" | custom-call | tf_op jit(solution)/shard_map/pallas_call | solution.py:843
  125.6 0.0 copy-done
  125.6 0.0 copy-done.1
  125.6 4.4 %shard_map.60 = (f32[1024,1024]{1,0:T(8,128)}, bf16[3,2,2,16,1024]{4,3,2,1,0:T(8,128)(2,1)}) custom-call(s32[2,24]{1,0:T(2,128)S(1)} %bitcast.8, bf16[40,4,2,2,16,1024]{5,4,3,2,1,0:T(8,128)(2,1)} %shard_map.59.results, f32[1024,1024]{1,0:T(8,128)S(1)} %bitcast.6), custom_call_target="tpu_custom_call" | custom-call | tf_op jit(solution)/shard_map/pallas_call | solution.py:899
Async XLA Ops:
  0.6 124.9 %copy-start = (f32[1,1,1,1024,1024]{4,3,2,1,0:T(8,128)S(1)}, f32[1,1,1,1024,1024]{4,3,2,1,0:T(8,128)}, u32[]{:S(2)}) copy-start(f32[1,1,1,1024,1024]{4,3,2,1,0:T(8,128)} %param.6) | copy-start | bytes 12582916
  0.6 124.9 %copy-start.1 = (s32[24,2]{0,1:T(2,128)S(1)}, s32[24,2]{0,1:T(2,128)}, u32[]{:S(2)}) copy-start(s32[24,2]{0,1:T(2,128)} %param.5) | copy-start | bytes 580

commit v4 on v2

--- a/solution.py
+++ b/solution.py
@@ -305,9 +305,8 @@
 
 
 def spot(s, block):
-    if block < 4:
-        return block, 0
-    return (block - 4, 1) if s == 0 else (block - 2, 1)
+    rank = lax.div(block, 4)
+    return block - (4, 2)[s] * rank, rank
 
 
 class Workers:
@@ -480,14 +479,20 @@
         self.add(own.at[s, i, part], terms, 3)
         self.ship(2, s, way, own.at[s, i, part], first_in.at[2, s, way])
 
-    def first_sum(self, s, j, b):
+    def first_sum(self, s, j, k, low):
         own, cin, first_in = self.v["own"], self.v["cin"], self.v["first_in"]
-        i = self.i[s][0]
+        i, b = self.i[s][0], 3 * low + k
         total = own[s, i, b, j].astype(f32) + cin[s, i, b, j].astype(f32)
-        k, low = (b, 0) if b < 3 else (b - 3, 1)
-        for stage, way in ((2, low), (1, 1 - low)):
-            total = total + first_in[stage, s, way, k, j].astype(f32)
-        return total
+        total = total + first_in[2, s, low, k, j].astype(f32)
+        return total + first_in[1, s, 1 - low, k, j].astype(f32)
+
+    def first_done(self, s, j):
+        f = self.v["f"]
+
+        @pl.loop(0, 3)
+        def _(k):
+            for low in range(2):
+                f[s, j, 3 * low + k] = self.first_sum(s, j, k, low).astype(bf16)
 
     def second(self, s):
         f, second_in = self.v["f"], self.v["second_in"]
@@ -496,8 +501,7 @@
             for way in range(2):
                 self.copies[stage, s, way].wait_recv()
         j = self.j[s][2]
-        for b in range(6):
-            f[s, j, b] = self.first_sum(s, j, b).astype(bf16)
+        self.first_done(s, j)
         self.ship(3, s, 0, f.at[s, j, lo], second_in.at[0, s, 0])
         self.ship(3, s, 1, f.at[s, j, hi], second_in.at[0, s, 1])
 
@@ -505,8 +509,7 @@
         f, second_in = self.v["f"], self.v["second_in"]
         o, part = ((1, hi), (3, lo))[way]
         j = self.j[s][o]
-        for b in range(6):
-            f[s, j, b] = self.first_sum(s, j, b).astype(bf16)
+        self.first_done(s, j)
         self.ship(4, s, way, f.at[s, j, part], second_in.at[1, s, way])
 
     def second_merged(self, way, s):
@@ -514,9 +517,12 @@
         o, part, start = ((1, lo, 0), (3, hi, 3))[way]
         j = self.j[s][o]
         self.copies[3, s, way].wait_recv()
-        for k in range(3):
+
+        @pl.loop(0, 3)
+        def _(k):
             total = f[s, j, start + k].astype(f32) + second_in[0, s, way, k].astype(f32)
             f[s, j, start + k] = total.astype(bf16)
+
         self.ship(5, s, way, f.at[s, j, part], second_in.at[2, s, way])
 
     def finish(self, s, out):
@@ -525,12 +531,14 @@
             for way in range(2):
                 self.copies[stage, s, way].wait_recv()
         j = self.j[s][0]
-        for b in range(6):
-            total = self.first_sum(s, j, b)
-            k, low = (b, 0) if b < 3 else (b - 3, 1)
-            total = total + second_in[2, s, low, k].astype(f32)
-            total = total + second_in[1, s, 1 - low, k].astype(f32)
-            out[b, s] = total.astype(bf16)
+
+        @pl.loop(0, 3)
+        def _(k):
+            for low in range(2):
+                total = self.first_sum(s, j, k, low)
+                total = total + second_in[2, s, low, k].astype(f32)
+                total = total + second_in[1, s, 1 - low, k].astype(f32)
+                out[3 * low + k, s] = total.astype(bf16)
 
 
 (
@@ -664,7 +672,9 @@
         for copy in kept["z", 1] + [kept["z", 2], kept["z", 3]]:
             copy.wait_recv()
         for side in range(2):
-            for block in range(6):
+
+            @pl.loop(0, 6)
+            def _(block, side=side):
                 where, rows = wanted(t, side * 6 + block)
                 away = wrap(where - t)
                 if side == 0:
@@ -690,9 +700,11 @@
         kept["g_pass", s, way] = net.start(rows, rows, right if way == 0 else left)
 
     def send_g(s):
-        for block in range(6):
+        @pl.loop(0, 6)
+        def _(block):
             line, rank = spot(s, block)
             g_send[s, line, 0, rank] = g[block, s]
+
         kept["gl", s] = WorkerLeg(net, s, g_send.at[s], g_mid.at[s], v["g_relay"].at[s])
 
     def send_roots(s):
@@ -770,9 +782,12 @@
     def _():
         for s in range(2):
             kept["ul", s].finish()
-            for block in range(6):
+
+            @pl.loop(0, 6)
+            def _(block, s=s):
                 line, rank = spot(s, block)
-                v["update"][block // 2, block % 2, s] = home[s, line, rank]
+                v["update"][lax.div(block, 2), lax.rem(block, 2), s] = home[s, line, rank]
+
         kept["update"] = net.local(v["update"], v["results"].at[4, pl.ds(0, 3)])
 
     steps[(OWE,)] = owned.finish
@@ -876,14 +891,26 @@
 
 def stats_kernel(owners, results, old_ref, new_ref, update_out, block, turned, stats, held, sem):
     me = lax.axis_index("dp") * 4 + lax.axis_index("tensor")
-    parts = [pl.ds(256 * i, 256) for i in range(4)]
     copy = pltpu.make_async_copy
-    fetches = [copy(results.at[i], block.at[i], sem.at[i]) for i in range(4)]
-    loads = [copy(old_ref.at[parts[i]], stats.at[parts[i]], sem.at[4 + i]) for i in range(4)]
-    stores = [copy(stats.at[parts[i]], new_ref.at[parts[i]], sem.at[8 + i]) for i in range(4)]
+
+    def part(i):
+        return pl.ds(pl.multiple_of(256 * i, 256), 256)
+
+    def fetch(i):
+        return copy(results.at[i], block.at[i], sem.at[i])
+
+    def load(i):
+        return copy(old_ref.at[part(i)], stats.at[part(i)], sem.at[4 + i])
+
+    def store(i):
+        return copy(stats.at[part(i)], new_ref.at[part(i)], sem.at[8 + i])
+
     take, give = copy(results.at[4, pl.ds(0, 3)], held, sem.at[12]), copy(held, update_out, sem.at[13])
-    for each in fetches + [take] + loads:
-        each.start()
+    for i in range(4):
+        fetch(i).start()
+    for i in range(4):
+        load(i).start()
+    take.start()
     is_left, is_right = owners[0, 0] == me, owners[1, 0] == me
     for b in range(1, 24):
         is_left = jnp.logical_or(is_left, owners[0, b] == me)
@@ -893,26 +920,31 @@
     def rows(i):
         return block[i].reshape(256, 1024)
 
-    def turn(i):
-        turned[:, parts[i]] = rows(i).T
-
-    for i in range(4):
-        fetches[i].wait()
-        pl.when(named)(functools.partial(turn, i))
+    @pl.loop(0, 4)
+    def _(i):
+        fetch(i).wait()
+
+        @pl.when(named)
+        def _():
+            turned[:, part(i)] = rows(i).T
+
     take.wait()
     give.start()
 
     def blend(i, some, other):
         gram = jnp.dot(some, other, preferred_element_type=f32)
-        stats[parts[i], :] = decay_rate * stats[parts[i], :] + (1 - decay_rate) * (gram * 1024 ** (-0.5))
+        stats[part(i), :] = decay_rate * stats[part(i), :] + (1 - decay_rate) * (gram * 1024 ** (-0.5))
+
+    @pl.loop(0, 4)
+    def _(i):
+        load(i).wait()
+        pl.when(is_left)(lambda: blend(i, rows(i), turned[...]))
+        pl.when(is_right)(lambda: blend(i, turned[part(i), :], block[...].reshape(1024, 1024)))
+        store(i).start()
 
     for i in range(4):
-        loads[i].wait()
-        pl.when(is_left)(lambda i=i: blend(i, rows(i), turned[...]))
-        pl.when(is_right)(lambda i=i: blend(i, turned[parts[i], :], block[...].reshape(1024, 1024)))
-        stores[i].start()
-    for each in stores + [give]:
-        each.wait()
+        store(i).wait()
+    give.wait()
 
 
 def finish_stats(owner_slots, results, old):

time: 131 us -> 132 us (level)
  no operation moved by 1% of the time
where the time goes in v4:
time: 132 us; the launch traced here: 130 us
  Pallas kernels  130 us (98%)
    pallas_call x1, Pallas kernels, step(): pl.pallas_call(functools.partial(step_kernel, names), out_shape=jax.Shape...  125 us
    pallas_call x1, Pallas kernels, finish_stats(): pl.pallas_call(stats_kernel, out_shape=(jax.ShapeDtypeStruct(old.shape, f...  4.51 us

profile of v4, /device:TPU:1, one launch (start us, length us, event | category | flops | bytes accessed | tf_op | source)
XLA Modules:
  0.0 130.3 jit_solution(10172771793338504925)
XLA Ops:
  0.6 0.0 copy-start
  0.6 0.0 copy-start.1
  0.7 125.1 %shard_map.59.results = bf16[40,4,2,2,16,1024]{5,4,3,2,1,0:T(8,128)(2,1)} custom-call(bf16[6,4,4,2,2,16,1024]{6,5,4,3,2,1,0:T(8,128)(2,1)} %bitcast.9, s32[2,24]{1,0:T(2,128)} %bitcast.7, bf16[4,4,2,2,16,1024]{5,4,3,2,1,0:T(8,128)(2,1)} %bitcast.10), custom_call_target="tpu_custom_call" | custom-call | tf_op jit(solution)/shard_map/pallas_call | solution.py:880
  125.7 0.0 copy-done
  125.7 0.0 copy-done.1
  125.8 4.5 %shard_map.60 = (f32[1024,1024]{1,0:T(8,128)}, bf16[3,2,2,16,1024]{4,3,2,1,0:T(8,128)(2,1)}) custom-call(s32[2,24]{1,0:T(2,128)S(1)} %bitcast.8, bf16[40,4,2,2,16,1024]{5,4,3,2,1,0:T(8,128)(2,1)} %shard_map.59.results, f32[1024,1024]{1,0:T(8,128)S(1)} %bitcast.6), custom_call_target="tpu_custom_call" | custom-call | tf_op jit(solution)/shard_map/pallas_call | solution.py:953
Async XLA Ops:
  0.6 125.1 %copy-start = (f32[1,1,1,1024,1024]{4,3,2,1,0:T(8,128)S(1)}, f32[1,1,1,1024,1024]{4,3,2,1,0:T(8,128)}, u32[]{:S(2)}) copy-start(f32[1,1,1,1024,1024]{4,3,2,1,0:T(8,128)} %param.6) | copy-start | bytes 12582916
  0.6 125.1 %copy-start.1 = (s32[24,2]{0,1:T(2,128)S(1)}, s32[24,2]{0,1:T(2,128)}, u32[]{:S(2)}) copy-start(s32[24,2]{0,1:T(2,128)} %param.5) | copy-start | bytes 580

commit v5 on v4

--- a/solution.py
+++ b/solution.py
@@ -44,6 +44,7 @@
         barrier = pltpu.get_barrier_semaphore()
         peers = [self.pair] + [self.near(axis, step) for axis in "xyz" for step in (1, -1)]
         peers += [self.near(axis, step, 1) for axis in "xy" for step in (1, -1)]
+        peers += [self.near(axis, 2) for axis in "xy"]
         for peer in peers:
             pl.semaphore_signal(barrier, inc=1, device_id=peer, device_id_type=MESH)
         pl.semaphore_wait(barrier, len(peers))
@@ -75,6 +76,9 @@
             else:
                 pl.when(when)(copy.wait_send)
         self.open = self.open[count:]
+
+
+ROUND = ((2, 2), (1, 1), (3, -1))
 
 
 class Exchange:
@@ -246,62 +250,27 @@
 
 
 class HomeLeg:
-    def __init__(self, net, s, back, home, relay):
-        self.net, self.axis, self.home, self.relay = net, "xy"[s], home, relay
-        here = net.at[self.axis]
-        self.i = i = [wrap(here + o) for o in range(4)]
+    def __init__(self, net, s, back, home):
+        axis = "xy"[s]
+        i = [wrap(net.at[axis] + o) for o in range(4)]
         self.two = [v < 2 if s == 0 else v >= 2 for v in i]
-        wide = relay.shape[-1]
-        self.cols = [pl.ds(0, wide), pl.ds(wide, wide)]
-        self.far = [
+        self.arrive = [
             [
                 net.start(
-                    back.at[rank, i[2], :, self.cols[way]],
-                    relay.at[way, rank],
-                    net.near(self.axis, 1 - 2 * way),
-                    self.when(0, rank),
+                    back.at[rank, i[o]], home.at[i[0], rank], net.near(axis, step), self.two[0] if rank else None
                 )
-                for way in range(2)
+                for o, step in ROUND
             ]
             for rank in range(2)
         ]
-        self.direct = [
-            [
-                net.start(back.at[rank, i[o]], home.at[i[0], rank], net.near(self.axis, step), self.when(0, rank))
-                for o, step in ((1, 1), (3, -1))
-            ]
-            for rank in range(2)
-        ]
         self.own = net.local(back.at[:, i[0]], home.at[i[0]])
-        self.passed = [[], []]
-
-    def when(self, o, rank):
-        return self.two[o] if rank else None
-
-    def arrived(self, copy, o, rank):
-        if rank:
-            pl.when(self.two[o])(copy.wait_recv)
-        else:
-            copy.wait_recv()
-
-    def forward(self, way):
-        o = (3, 1)[way]
-        for rank in range(2):
-            self.arrived(self.far[rank][way], o, rank)
-            self.passed[rank].append(
-                self.net.start(
-                    self.relay.at[way, rank],
-                    self.home.at[self.i[o], rank, :, self.cols[way]],
-                    self.net.near(self.axis, 1 - 2 * way),
-                    self.when(o, rank),
-                )
-            )
 
     def finish(self):
         self.own.wait()
-        for rank in range(2):
-            for copy, o in zip(self.direct[rank] + self.passed[rank], (3, 1, 2, 2)):
-                self.arrived(copy, o, rank)
+        for copy in self.arrive[0]:
+            copy.wait_recv()
+        for copy, source in zip(self.arrive[1], (2, 3, 1)):
+            pl.when(self.two[source])(copy.wait_recv)
 
 
 def spot(s, block):
@@ -320,6 +289,9 @@
     def rank(self, s, step):
         i, j = self.ij[s]
         return lax.div(wrap(j + step - i), 2)
+
+    def around(self, s):
+        return [self.net.near(self.axes[s], step) for _, step in ROUND]
 
     def beside(self, s):
         return self.net.near(self.axes[s], 1), self.net.near(self.axes[s], -1)
@@ -372,49 +344,31 @@
 
 
 class Spread:
-    def __init__(self, w, s, unit, land, relay):
+    def __init__(self, w, s, unit, land):
         self.w, net = w, w.net
-        right, left = w.beside(s)
         j = [wrap(w.ij[s][1] + o) for o in range(4)]
-        mine = w.rank(s, 0)
-        self.far = [net.make(unit(j[2], 0), relay.at[0], right), net.make(unit(j[2], 1), relay.at[1], left)]
-        self.direct = [
-            net.make(unit(j[1], None), land(mine, None), right),
-            net.make(unit(j[3], None), land(mine, None), left),
-        ]
-        self.passed = [
-            net.make(relay.at[0], land(w.rank(s, 3), 0), right),
-            net.make(relay.at[1], land(w.rank(s, 1), 1), left),
-        ]
-        self.own = pltpu.make_async_copy(unit(j[0], None), land(mine, None), net.send.at[net.count])
+        here = land(w.rank(s, 0))
+        self.sent = [net.make(unit(j[o]), here, device) for (o, _), device in zip(ROUND, w.around(s))]
+        self.own = pltpu.make_async_copy(unit(j[0]), here, net.send.at[net.count])
         net.count += 1
 
         @pl.when(w.is_worker)
         def _():
-            for copy in self.far + self.direct + [self.own]:
+            for copy in self.sent + [self.own]:
                 copy.start()
 
-        net.open += [(copy, w.is_worker) for copy in self.far + self.direct]
-        net.open += [(copy, w.is_other) for copy in self.passed]
-
-    def forward(self):
-        @pl.when(self.w.is_other)
-        def _():
-            for arrived, onward in zip(self.far, self.passed):
-                arrived.wait_recv()
-                onward.start()
+        net.open += [(copy, w.is_worker) for copy in self.sent]
 
     def finish(self):
         @pl.when(self.w.is_other)
         def _():
-            for copy in self.direct:
+            for copy in self.sent[1:]:
                 copy.wait_recv()
 
         @pl.when(self.w.is_worker)
         def _():
             self.own.wait()
-            for copy in self.passed:
-                copy.wait_recv()
+            self.sent[0].wait_recv()
 
 
 class ReduceScatter:
@@ -543,9 +497,9 @@
 
 (
     BLK, FAR, FETCH, G, GG, GGF, GL, GLF, MERGED, MMA, MMB, OW1, OW1F, OW2, OW2F, OWE, PLAIN, RG, RGF, RL, RLF,
-    RO1, RO1F, RO2, RO2F, SEC, SECM, SECP, SH0, SH1, SP, SPF, UL, ULE, ULF, ZAF, ZF, ZM, ZP, ZSEL,
-) = range(40)
-CLOSING = (ULF, 0, 1)
+    RO1, RO1F, RO2, RO2F, SEC, SECM, SECP, SH0, SH1, SP, UL, ULE, ZAF, ZF, ZM, ZP, ZSEL,
+) = range(38)
+CLOSING = (OW2F, 0, 0)
 RESULTS = 40
 ORDER = (
     (RO1, 1), (RO1, 0), (BLK,), (RO1F, 1, 1), (RO1F, 0, 1), (RO1F, 1, 0), (RO1F, 0, 0), (FETCH,), (RO2, 1),
@@ -556,8 +510,8 @@
     (G, 1), (GL, 0), (RLF, 1, 1), (GL, 1), (RLF, 1, 0), (GLF, 1, 0), (GLF, 0, 0), (RLF, 0, 0), (GLF, 0, 1),
     (GLF, 1, 1), (RLF, 0, 1), (RG, 1), (GG, 0), (GGF, 0), (ZAF, 0, 0), (ZAF, 0, 1), (ZAF, 1, 1), (RG, 0),
     (GG, 1), (GGF, 1), (ZAF, 1, 0), (RGF, 1), (OW1, 0), (RGF, 0), (OW1, 1), (SH0,), (SH1,), (MMA,),
-    (OW1F, 0, 0), (OW1F, 0, 1), (OW1F, 1, 0), (OW1F, 1, 1), (MMB,), (SP,), (SPF, 0), (SPF, 1), (OW2, 1),
-    (OW2, 0), (UL, 0), (OW2F, 1, 0), (UL, 1), (ULF, 0, 1), (ULF, 1, 0), (ULF, 0, 0), (OW2F, 0, 0), (ULF, 1, 1),
+    (OW1F, 0, 0), (OW1F, 0, 1), (OW1F, 1, 0), (OW1F, 1, 1), (MMB,), (SP,), (OW2, 1),
+    (OW2, 0), (UL, 0), (OW2F, 1, 0), (UL, 1), (OW2F, 0, 0),
     (OW2F, 1, 1), (OW2F, 0, 1), (ULE,), (OWE,),
 )
 
@@ -769,14 +723,13 @@
             kept["sp", s] = Spread(
                 workers,
                 s,
-                lambda j, h, s=s: result.at[half(h), j, 0] if s == 0 else result.at[j, half(h), 1],
-                lambda rank, h, s=s: back.at[s, rank, half(h)],
-                v["u_relay"].at[s],
+                lambda j, s=s: result.at[:, j, 0] if s == 0 else result.at[j, :, 1],
+                lambda rank, s=s: back.at[s, rank],
             )
 
     def go_home(s):
         kept["sp", s].finish()
-        kept["ul", s] = HomeLeg(net, s, back.at[s], home.at[s], v["u_relay2"].at[s])
+        kept["ul", s] = HomeLeg(net, s, back.at[s], home.at[s])
 
     @step((ULE,))
     def _():
@@ -808,7 +761,6 @@
         steps[RG, s] = bind(gather, "rg", "rl", s, root_mid, 0, 2, v["r_relay2"])
         steps[GGF, s] = lambda s=s: kept["gg", s].forward()
         steps[RGF, s] = lambda s=s: kept["rg", s].forward()
-        steps[SPF, s] = lambda s=s: kept["sp", s].forward()
         steps[UL, s] = bind(go_home, s)
         for way in range(2):
             steps[PLAIN, way, s] = bind(sums.plain, way, s)
@@ -820,7 +772,7 @@
                 steps[name, s, way] = (
                     lambda trip=trip, leg=leg, s=s, way=way: trip.legs[leg, s].forward(way)
                 )
-            for name, leg in ((GLF, "gl"), (RLF, "rl"), (ULF, "ul")):
+            for name, leg in ((GLF, "gl"), (RLF, "rl")):
                 steps[name, s, way] = lambda leg=leg, s=s, way=way: kept[leg, s].forward(way)
     assert sorted(steps) == sorted(ORDER)
     for name in ORDER:
@@ -865,12 +817,10 @@
         "back": (2, 2, 4),
         "home": (2, 4, 2),
         "update": (3, 2, 2),
-        "u_relay": (2, 2, 2),
     }
     scratch = {name: pltpu.VMEM(shape + tile, bf16) for name, shape in vmem.items()}
     scratch["g_relay"] = pltpu.VMEM((2, 2, 1, 2, 16, tile[1] // 2), bf16)
     scratch["r_relay"] = pltpu.VMEM((2, 2, 2, 2, 16, tile[1] // 2), bf16)
-    scratch["u_relay2"] = pltpu.VMEM((2, 2, 2, 16, tile[1] // 2), bf16)
     scratch["mixed"] = pltpu.VMEM((512, tile[1]), bf16)
     scratch["blocks"] = pltpu.SMEM((32,), jnp.int32)
     scratch["send"] = pltpu.SemaphoreType.DMA((256,))
@@ -899,17 +849,15 @@
     def fetch(i):
         return copy(results.at[i], block.at[i], sem.at[i])
 
-    def load(i):
-        return copy(old_ref.at[part(i)], stats.at[part(i)], sem.at[4 + i])
+    load = copy(old_ref, stats, sem.at[4])
 
     def store(i):
-        return copy(stats.at[part(i)], new_ref.at[part(i)], sem.at[8 + i])
+        return copy(stats.at[:, part(i)], new_ref.at[:, part(i)], sem.at[8 + i])
 
     take, give = copy(results.at[4, pl.ds(0, 3)], held, sem.at[12]), copy(held, update_out, sem.at[13])
     for i in range(4):
         fetch(i).start()
-    for i in range(4):
-        load(i).start()
+    load.start()
     take.start()
     is_left, is_right = owners[0, 0] == me, owners[1, 0] == me
     for b in range(1, 24):
@@ -933,13 +881,14 @@
 
     def blend(i, some, other):
         gram = jnp.dot(some, other, preferred_element_type=f32)
-        stats[part(i), :] = decay_rate * stats[part(i), :] + (1 - decay_rate) * (gram * 1024 ** (-0.5))
+        stats[:, part(i)] = decay_rate * stats[:, part(i)] + (1 - decay_rate) * (gram * 1024 ** (-0.5))
+
+    load.wait()
 
     @pl.loop(0, 4)
     def _(i):
-        load(i).wait()
-        pl.when(is_left)(lambda: blend(i, rows(i), turned[...]))
-        pl.when(is_right)(lambda: blend(i, turned[part(i), :], block[...].reshape(1024, 1024)))
+        pl.when(is_left)(lambda: blend(i, block[...].reshape(1024, 1024), turned[:, part(i)]))
+        pl.when(is_right)(lambda: blend(i, turned[...], block[:, :, :, :, :, part(i)].reshape(1024, 256)))
         store(i).start()
 
     for i in range(4):

time: 132 us -> 131 us (level); the launches traced: 130 us -> 131 us
  no operation moved by 1% of the time
where the time goes in v5:
time: 131 us
  Pallas kernels  130 us (99%)
    pallas_call x1, Pallas kernels, step(): pl.pallas_call(functools.partial(step_kernel, names), out_shape=jax.Shape...  125 us
    pallas_call x1, Pallas kernels, finish_stats(): pl.pallas_call(stats_kernel, out_shape=(jax.ShapeDtypeStruct(old.shape, f...  4.5 us

profile of v5, /device:TPU:1, one launch (start us, length us, event | category | flops | bytes accessed | tf_op | source)
XLA Modules:
  0.0 130.6 jit_solution(12638249624711760467)
XLA Ops:
  0.6 0.0 copy-start
  0.6 0.0 copy-start.1
  0.7 125.4 %shard_map.59.results = bf16[40,4,2,2,16,1024]{5,4,3,2,1,0:T(8,128)(2,1)} custom-call(bf16[6,4,4,2,2,16,1024]{6,5,4,3,2,1,0:T(8,128)(2,1)} %bitcast.9, s32[2,24]{1,0:T(2,128)} %bitcast.7, bf16[4,4,2,2,16,1024]{5,4,3,2,1,0:T(8,128)(2,1)} %bitcast.10), custom_call_target="tpu_custom_call" | custom-call | tf_op jit(solution)/shard_map/pallas_call | solution.py:830
  126.1 0.0 copy-done
  126.1 0.0 copy-done.1
  126.1 4.5 %shard_map.60 = (f32[1024,1024]{1,0:T(8,128)}, bf16[3,2,2,16,1024]{4,3,2,1,0:T(8,128)(2,1)}) custom-call(s32[2,24]{1,0:T(2,128)S(1)} %bitcast.8, bf16[40,4,2,2,16,1024]{5,4,3,2,1,0:T(8,128)(2,1)} %shard_map.59.results, f32[1024,1024]{1,0:T(8,128)S(1)} %bitcast.6), custom_call_target="tpu_custom_call" | custom-call | tf_op jit(solution)/shard_map/pallas_call | solution.py:902
Async XLA Ops:
  0.6 125.5 %copy-start = (f32[1,1,1,1024,1024]{4,3,2,1,0:T(8,128)S(1)}, f32[1,1,1,1024,1024]{4,3,2,1,0:T(8,128)}, u32[]{:S(2)}) copy-start(f32[1,1,1,1024,1024]{4,3,2,1,0:T(8,128)} %param.6) | copy-start | bytes 12582916
  0.6 125.5 %copy-start.1 = (s32[24,2]{0,1:T(2,128)S(1)}, s32[24,2]{0,1:T(2,128)}, u32[]{:S(2)}) copy-start(s32[24,2]{0,1:T(2,128)} %param.5) | copy-start | bytes 580
